TPU v7x, 32 devices: a whole 2x2x4 slice. The times are simulated.
32 devices in a mesh: seq: 16 (over z, y, x), head: 2 (over core).
Axes of the slice: x: 2, y: 2, z: 4, core: 2. Of those that a mesh axis runs over, the one named last changes fastest.
Arguments:
- queries: bfloat16 [2048, 6144], P('seq', 'head'), may hold values from -6 to 6
- key_vectors: bfloat16 [2048, 6144], P('seq', 'head'), may hold values from -6 to 6
- value_vectors: bfloat16 [2048, 6144], P('seq', 'head'), may hold values from -6 to 6
- norm_gain: float32 [6144], P('head'), may hold values from 0.1 to 1.9
- upstream: bfloat16 [2048, 6144], P('seq', 'head'), may hold values from -6 to 6
Outputs:
- attended: bfloat16 [2048, 6144], P('seq', 'head')
- grad_queries: bfloat16 [2048, 6144], P('seq', 'head')
- grad_keys: bfloat16 [2048, 6144], P('seq', 'head')
- grad_values: bfloat16 [2048, 6144], P('seq', 'head')
- grad_gain: float32 [6144], P('head')
All inputs are finite; a program needn't handle non-finite values.
Results may differ from a plain program's by a relative error of at most 0.0058.
Values may be sent and summed in bfloat16 or wider, within the bound.
No kernel may reach another device: no remote copies, remote signals or barrier semaphores. Data moves between devices by JAX's collectives and lax.ppermute only.
A program may use at most 64 MiB of HBM per device.

v0:
```python
import jax
import jax.numpy as jnp
from jax import lax
from jax.sharding import PartitionSpec as P

HEADS = 48
HEAD_DIM = 128


def prefix(part, axis, combine, identity):
    count = lax.axis_size(axis)
    place = lax.axis_index(axis)
    ahead = count - 1 - place
    gathered = lax.all_gather(part, axis)
    state = jnp.zeros_like(part) + jnp.asarray(identity, part.dtype)

    def one(lap, state):
        source = count - 1 - lap
        return combine(state, lax.dynamic_index_in_dim(gathered, source, 0, False))

    return lax.fori_loop(0, ahead, one, state)


def split_shares(state):
    count = lax.axis_size("seq")
    return state.reshape(count, 1, -1)


def share_running(received):
    empty = jnp.zeros_like(received[:, :1])
    summed = jnp.cumsum(received, axis=1)
    return jnp.concatenate([empty, summed[:, :-1]], axis=1)


def body(queries, key_vectors, value_vectors, norm_gain, upstream):
    length = queries.shape[0]
    head_count = queries.shape[1] // HEAD_DIM
    total_width = HEADS * HEAD_DIM
    shaped = (length, head_count, HEAD_DIM)
    query_rows = queries.reshape(shaped)
    key_rows = key_vectors.reshape(shaped)
    value_rows = value_vectors.reshape(shaped)
    upstream_f = upstream.reshape(shaped).astype(jnp.float32)
    gain_grid = norm_gain.reshape(head_count, HEAD_DIM)
    positions = jnp.arange(length, dtype=jnp.int32)
    causal = (positions[None, :] <= positions[:, None])[None]
    local_state = jnp.einsum(
        "thd,the->hde", key_rows, value_rows, preferred_element_type=jnp.float32
    )
    moved = lax.all_to_all(
        split_shares(local_state), "seq", split_axis=0, concat_axis=1, tiled=True
    )
    rounded = share_running(moved).astype(jnp.bfloat16)
    returned = lax.all_to_all(rounded, "seq", split_axis=1, concat_axis=0, tiled=True)
    prior_b = returned.reshape(local_state.shape)
    scores = jnp.einsum("thd,shd->hts", query_rows, key_rows, preferred_element_type=jnp.float32)
    weights = jnp.where(causal, scores, 0.0).astype(jnp.bfloat16)
    out = jnp.einsum("hts,she->the", weights, value_rows, preferred_element_type=jnp.float32)
    out = out + jnp.einsum("thd,hde->the", query_rows, prior_b, preferred_element_type=jnp.float32)
    grad_norm = upstream_f * gain_grid
    square_total = lax.psum(jnp.sum(out * out, axis=(1, 2)), "head")
    inv = lax.rsqrt(square_total / total_width + 1e-06)[:, None, None]
    scaled = out * inv
    dot_total = lax.psum(jnp.sum(grad_norm * scaled, axis=(1, 2)), "head")
    mean_dot = (dot_total / total_width)[:, None, None]
    attended = (scaled * gain_grid).astype(jnp.bfloat16).reshape(length, -1)
    d_out = (inv * (grad_norm - scaled * mean_dot)).astype(jnp.bfloat16)
    gain_part = jnp.sum(upstream_f * scaled, axis=0).reshape(-1)
    grad_state = jnp.einsum("thd,the->hde", query_rows, d_out, preferred_element_type=jnp.float32)
    later = prefix(grad_state, "seq", jnp.add, jnp.zeros_like(grad_state))
    grad_gain = lax.psum(gain_part, "seq")
    later_b = later.astype(jnp.bfloat16)
    d_scores = jnp.einsum("the,she->hts", d_out, value_rows, preferred_element_type=jnp.float32)
    d_scores = jnp.where(causal, d_scores, 0.0).astype(jnp.bfloat16)
    grad_q = jnp.einsum("hts,shd->thd", d_scores, key_rows, preferred_element_type=jnp.float32)
    grad_q = grad_q + jnp.einsum("the,hde->thd", d_out, prior_b, preferred_element_type=jnp.float32)
    grad_k = jnp.einsum("hts,thd->shd", d_scores, query_rows, preferred_element_type=jnp.float32)
    grad_k = grad_k + jnp.einsum(
        "she,hde->shd", value_rows, later_b, preferred_element_type=jnp.float32
    )
    grad_v = jnp.einsum("hts,the->she", weights, d_out, preferred_element_type=jnp.float32)
    grad_v = grad_v + jnp.einsum(
        "shd,hde->she", key_rows, later_b, preferred_element_type=jnp.float32
    )
    return (
        attended,
        grad_q.astype(jnp.bfloat16).reshape(length, -1),
        grad_k.astype(jnp.bfloat16).reshape(length, -1),
        grad_v.astype(jnp.bfloat16).reshape(length, -1),
        grad_gain,
    )


def solution(mesh):
    in_specs = (P("seq", "head"), P("seq", "head"), P("seq", "head"), P("head"), P("seq", "head"))
    out_specs = (P("seq", "head"), P("seq", "head"), P("seq", "head"), P("seq", "head"), P("head"))
    return jax.shard_map(body, mesh=mesh, in_specs=in_specs, out_specs=out_specs, check_vma=False)
```

profile of v0, /device:TPU:1, one launch (start us, length us, event | category | flops | bytes accessed | tf_op | source)
XLA Modules:
  0.0 435.7 jit_solution(15541217318832840052)
XLA Ops:
  10.0 43.0 %all_to_all.21 = f32[16,1,24576]{2,1,0:T(1,128)S(1)} all-to-all(f32[16,1,24576]{2,1,0:T(1,128)S(1)} %bitcast.114), channel_id=1, replica_groups=mesh['seq'=16,'head'=2] {'seq'}, dimensions={0} | all-to-all | bytes 3145728 | tf_op jit(solution)/shard_map/all_to_all | solution.py:50
  53.9 2.2 reduce_window_sum.11
  56.1 2.5 copy.83
  60.8 6.3 %reduce.2 = bf16[16,24576]{1,0:T(8,128)(2,1)} reduce(bf16[16,1,24576]{2,1,0:T(2,128)(2,1)S(1)} %pad_bitcast_fusion, bf16[]{:T(256)} %broadcast.18), dimensions={1}, to_apply=%pad_bitcast_fusion.reduce_sub_computation | reduce | bytes 1572866
  67.1 2.6 reshape.78
  69.7 5.0 %all-to-all-start.1 = ((bf16[16,2,12288]{2,1,0:T(2,128)(2,1)}), bf16[16,2,12288]{2,1,0:T(2,128)(2,1)}, u32[]{:S(2)}, u32[]{:S(2)}) async-start(bf16[16,2,12288]{2,1,0:T(2,128)(2,1)} %reshape.78), calls=%async_computation.1 | async-start | bytes 1572864 | tf_op jit(solution)/shard_map/all_to_all | solution.py:54
  79.1 1.9 fusion.2
  81.0 9.4 %all-to-all-done.1 = bf16[16,2,12288]{2,1,0:T(2,128)(2,1)} async-done(((bf16[16,2,12288]{2,1,0:T(2,128)(2,1)}), bf16[16,2,12288]{2,1,0:T(2,128)(2,1)}, u32[]{:S(2)}, u32[]{:S(2)}) %all-to-all-start.1) | async-done | bytes 786464 | tf_op jit(solution)/shard_map/all_to_all | solution.py:54
  90.4 5.2 %reshape.79 = bf16[16,1,24576]{2,1,0:T(2,128)(2,1)} reshape(bf16[16,2,12288]{2,1,0:T(2,128)(2,1)} %all-to-all-done.1) | data formatting | bytes 1572864
  95.6 6.8 %bitcast_reduce_fusion = bf16[16,24576]{1,0:T(8,128)(2,1)} fusion(bf16[16,1,24576]{2,1,0:T(2,128)(2,1)} %reshape.79), kind=kLoop, calls=%fused_computation.44 | loop fusion | bytes 1572864 | tf_op jit(solution)/shard_map/all_to_all | solution.py:54
  104.0 3.4 multiply_reduce_fusion.2
  107.4 7.2 %psum.21 = f32[128]{0:T(128)S(1)} all-reduce(f32[128]{0:T(128)S(1)} %get-tuple-element.97), channel_id=1, replica_groups=mesh['seq'=16,'head'=2] {'head'}, use_global_device_ids=true, to_apply=%region_2.3 | all-reduce | flops 128 | bytes 1024 | tf_op jit(solution)/shard_map/psum | solution.py:61
  114.6 2.3 multiply_reduce_fusion
  116.9 2.5 psum.22
  119.4 2.9 multiply_convert_fusion
  130.7 63.5 %psum.23 = f32[3072]{0:T(1024)} all-reduce(f32[3072]{0:T(1024)S(1)} %bitcast.123), channel_id=1, replica_groups=mesh['seq'=16,'head'=2] {'seq'}, use_global_device_ids=true, to_apply=%region_8.9 | all-reduce | flops 3072 | bytes 24576 | tf_op jit(solution)/shard_map/psum | solution.py:71
  195.8 199.8 %all-gather.3.cloned.1.call-done = f32[384,128,128]{2,1,0:T(8,128)} async-done(((f32[24,128,128]{2,1,0:T(8,128)}), f32[384,128,128]{2,1,0:T(8,128)}) %all-gather.3.cloned.1.call-update) | async-done | bytes 25165840 | tf_op jit(solution)/shard_map/all_gather | solution.py:14
  395.7 27.6 %while.12 = (s32[]{:T(128)}, f32[24,128,128]{2,1,0:T(8,128)S(1)}, s32[]{:T(128)}, f32[16,24,128,128]{3,2,1,0:T(8,128)}, s32[]{:T(128)}, /*index=5*/s32[]{:T(128)}, s32[]{:T(128)}, s32[]{:T(128)}) while((s32[]{:T(128)}, f32[24,128,128]{2,1,0:T(8,128)S(1)}, s32[]{:T(128)}, f32[16,24,128,128]{3,2,1,0:T(8,128)}, s32[]{:T(128)}, ...), condition=%wide.region_6.7_spmd, body=%wide.region_5.6_spmd.sunk | while | flops 393222 | bytes 4718735 | solution.py:21
  395.8 1.9 bitcast_add_fusion.5
  397.7 1.8 bitcast_add_fusion.5
  399.5 1.8 bitcast_add_fusion.5
  403.2 1.8 bitcast_add_fusion.5
  405.0 1.8 bitcast_add_fusion.5
  406.8 1.8 bitcast_add_fusion.5
  (69 shorter events, 43.6 us)
Async XLA Ops:
  7.2 69.2 %copy-start = (bf16[128,3072]{1,0:T(8,128)(2,1)S(1)}, bf16[128,3072]{1,0:T(8,128)(2,1)}, u32[]{:S(2)}) copy-start(bf16[128,3072]{1,0:T(8,128)(2,1)} %param.7) | copy-start | bytes 2359300
  7.2 2.0 copy-start.5
  9.1 0.9 copy-start.1
  69.7 20.7 %all-to-all-start.1 = ((bf16[16,2,12288]{2,1,0:T(2,128)(2,1)}), bf16[16,2,12288]{2,1,0:T(2,128)(2,1)}, u32[]{:S(2)}, u32[]{:S(2)}) async-start(bf16[16,2,12288]{2,1,0:T(2,128)(2,1)} %reshape.78), calls=%async_computation.1 | async-start | bytes 1572864 | tf_op jit(solution)/shard_map/all_to_all | solution.py:54
  74.7 320.9 %all-gather.3.cloned.1.call-start = ((), (), s32[]{:S(2)}) async-start(), calls=%async_computation.2 | async-start | bytes 26738688 | tf_op jit(solution)/shard_map/all_gather | solution.py:14
  78.2 0.9 copy-start.10
  103.9 3.5 copy-start.3
  104.0 10.6 %copy-start.15 = (f32[3072]{0:T(1024)S(1)}, f32[3072]{0:T(1024)}, u32[]{:S(2)}) copy-start(f32[3072]{0:T(1024)} %param.10) | copy-start | bytes 36868
  124.3 1.1 copy-start.12
  124.3 2.3 copy-start.6
  126.6 1.1 copy-start.2
  127.7 0.9 copy-start.13
  127.7 1.4 copy-start.4
  129.5 64.7 %copy-start.11 = (bf16[24,128,128]{2,1,0:T(8,128)(2,1)S(1)}, bf16[24,128,128]{2,1,0:T(8,128)(2,1)}, u32[]{:S(2)}) copy-start(bf16[24,128,128]{2,1,0:T(8,128)(2,1)} %copy-done.10) | copy-start | bytes 2359300
  395.7 27.7 %copy-start.7 = (bf16[128,3072]{1,0:T(8,128)(2,1)S(1)}, bf16[128,3072]{1,0:T(8,128)(2,1)}, u32[]{:S(2)}) copy-start(bf16[128,3072]{1,0:T(8,128)(2,1)} %param.9) | copy-start | bytes 2359300
  423.4 1.4 copy-start.8
  423.4 1.6 copy-start.9
  425.0 1.1 copy-start.14
Sparse Core Ops, SparseCore 0:
  124.4 271.0 all-gather.2
where the time goes:
time: 438 us; the launch traced here: 436 us
  waiting for transfers between devices  209 us (48%)
  blocking collectives  116 us (26%)
  other arithmetic  41 us (9%)
  local copies, waits for them, and re-layouts  36.6 us (8%)
  between operations  14.3 us (3%)
  matrix products  13 us (3%)
  starting transfers between devices  5.24 us (1%)
    all_gather x1, waiting for transfers between devices, prefix(): gathered = lax.all_gather(part, axis)  200 us
    psum x1, blocking collectives, body(): grad_gain = lax.psum(gain_part, 'seq')  63.5 us
    all_to_all x1, blocking collectives, body(): lax.all_to_all(split_shares(local_state), 'seq', split_axis=0, concat_axi...  43 us
    add x15, other arithmetic, one(): return combine(state, lax.dynamic_index_in_dim(gathered, source, 0, False))  27.3 us
    unnamed x42, local copies, waits for them, and re-layouts  23.6 us
    all_to_all x1, waiting for transfers between devices, body(): lax.all_to_all(rounded, 'seq', split_axis=1, concat_axis=0, tiled=True)  9.44 us
  transfers between devices with their start and end apart: 2, of which 2 were waited for; matrix products, arithmetic and copies ran while one was open for 2% of the time, Pallas kernels for 0%

commit v1 on v0

v1 whole, which is shorter than its diff:
```python
import functools

import jax
import jax.numpy as jnp
from jax import lax
from jax.experimental import pallas as pl
from jax.experimental.pallas import tpu as pltpu
from jax.sharding import PartitionSpec as P

HEAD_DIM = 128
F32 = jnp.float32
BF16 = jnp.bfloat16
VMEM_LIMIT = 24 * 1024 * 1024


def call(kernel, out_shape, *args):
    whole = pl.BlockSpec(memory_space=pltpu.VMEM)
    return pl.pallas_call(
        kernel,
        out_shape=out_shape,
        in_specs=[whole] * len(args),
        out_specs=jax.tree.map(lambda _: whole, out_shape),
        compiler_params=pltpu.CompilerParams(vmem_limit_bytes=VMEM_LIMIT),
    )(*args)


def shape(dims, dtype):
    return jax.ShapeDtypeStruct(dims, dtype)


def dot(a, b, over):
    return lax.dot_general(a, b, ((over[:1], over[1:]), ((), ())), preferred_element_type=F32)


def split(value):
    high = value.astype(BF16)
    return high, (value - high.astype(F32)).astype(BF16)


def columns(head):
    return pl.ds(head * HEAD_DIM, HEAD_DIM)


def causal_mask(length):
    rows = lax.broadcasted_iota(jnp.int32, (length, length), 0)
    cols = lax.broadcasted_iota(jnp.int32, (length, length), 1)
    return cols <= rows


def state_kernel(heads, key_ref, value_ref, state_ref):
    for h in range(heads):
        part = dot(key_ref[:, columns(h)], value_ref[:, columns(h)], (0, 0))
        state_ref[columns(h), :] = part.astype(BF16)


def weights_kernel(heads, query_ref, key_ref, value_ref, weights_ref, inner_ref):
    mask = causal_mask(query_ref.shape[0])
    for h in range(heads):
        scores = dot(query_ref[:, columns(h)], key_ref[:, columns(h)], (1, 1))
        weights = jnp.where(mask, scores, 0.0).astype(BF16)
        weights_ref[h] = weights
        inner_ref[:, columns(h)] = dot(weights, value_ref[:, columns(h)], (1, 0))


def out_kernel(heads, query_ref, prior_ref, inner_ref, up_ref, gain_ref, out_ref, sums_ref):
    squares = jnp.zeros(sums_ref.shape[1:], F32)
    products = jnp.zeros(sums_ref.shape[1:], F32)
    for h in range(heads):
        out = inner_ref[:, columns(h)] + dot(query_ref[:, columns(h)], prior_ref[columns(h), :], (1, 0))
        out_ref[:, columns(h)] = out
        squares += out * out
        products += up_ref[:, columns(h)].astype(F32) * gain_ref[h][None] * out
    sums_ref[0] = squares
    sums_ref[1] = products


def token_factors(total_width, sums_refs):
    sums = functools.reduce(lambda a, b: a + b, [ref[...] for ref in sums_refs])
    inv = lax.rsqrt(jnp.sum(sums[0], axis=1, keepdims=True) / total_width + 1e-6)
    mean_dot = jnp.sum(sums[1], axis=1, keepdims=True) / total_width * inv
    return inv, mean_dot


def grad_out_kernel(heads, total_width, parts, *refs):
    out_ref, up_ref, gain_ref, query_ref, *sums_refs = refs[:-2]
    grad_ref, sent_ref = refs[-2:]
    inv, mean_dot = token_factors(total_width, sums_refs)
    rows = heads * HEAD_DIM // parts
    sent_ref[:, rows:, :] = jnp.zeros((parts, sent_ref.shape[1] - rows, HEAD_DIM), BF16)
    gains = []
    for h in range(heads):
        scaled = out_ref[:, columns(h)] * inv
        up = up_ref[:, columns(h)].astype(F32)
        grad = (inv * (up * gain_ref[h][None] - scaled * mean_dot)).astype(BF16)
        grad_ref[:, columns(h)] = grad
        state = dot(query_ref[:, columns(h)], grad, (0, 0)).astype(BF16)
        at = 0
        while at < HEAD_DIM:
            part, row = divmod(h * HEAD_DIM + at, rows)
            count = min(HEAD_DIM - at, rows - row)
            sent_ref[part, row:row + count, :] = state[at:at + count]
            at += count
        gains.append(jnp.sum(up * scaled, axis=0, keepdims=True))
    high, low = split(jnp.concatenate(gains, axis=0))
    for part in range(parts):
        sent_ref[part, rows:rows + heads, :] = high
        sent_ref[part, rows + heads:rows + 2 * heads, :] = low


def inner_grads_kernel(heads, total_width, *refs):
    (query_ref, key_ref, value_ref, gain_ref, out_ref, weights_ref, grad_ref, prior_ref,
     *sums_refs) = refs[:-4]
    attended_ref, grad_q_ref, inner_k_ref, inner_v_ref = refs[-4:]
    inv, _ = token_factors(total_width, sums_refs)
    mask = causal_mask(query_ref.shape[0])
    for h in range(heads):
        cols = columns(h)
        attended_ref[:, cols] = (out_ref[:, cols] * inv * gain_ref[h][None]).astype(BF16)
        grad = grad_ref[:, cols]
        scores = dot(grad, value_ref[:, cols], (1, 1))
        scores = jnp.where(mask, scores, 0.0).astype(BF16)
        grad_q = dot(scores, key_ref[:, cols], (1, 0)) + dot(grad, prior_ref[cols, :], (1, 1))
        grad_q_ref[:, cols] = grad_q.astype(BF16)
        inner_k_ref[:, cols] = dot(scores, query_ref[:, cols], (0, 0))
        inner_v_ref[:, cols] = dot(weights_ref[h], grad, (0, 0))


def last_grads_kernel(heads, key_ref, value_ref, later_ref, inner_k_ref, inner_v_ref, grad_k_ref, grad_v_ref):
    for h in range(heads):
        cols = columns(h)
        later = later_ref[cols, :]
        grad_k = inner_k_ref[:, cols] + dot(value_ref[:, cols], later, (1, 1))
        grad_k_ref[:, cols] = grad_k.astype(BF16)
        grad_v = inner_v_ref[:, cols] + dot(key_ref[:, cols], later, (1, 0))
        grad_v_ref[:, cols] = grad_v.astype(BF16)


def total_kernel(rows, heads, got_ref, total_ref):
    total = jnp.sum(got_ref[:, :rows, :].astype(F32), axis=0)
    total_ref[:rows, :] = total.astype(BF16)
    if heads:
        total_ref[rows:, :] = jnp.zeros((total_ref.shape[0] - rows, HEAD_DIM), BF16)
        high, low = split(gain_sum(rows, heads, got_ref))
        total_ref[rows:rows + heads, :] = high
        total_ref[rows + heads:rows + 2 * heads, :] = low


def gain_sum(rows, heads, ref):
    both = jnp.sum(ref[:, rows:rows + 2 * heads, :].astype(F32), axis=0)
    return both[:heads] + both[heads:]


def running_kernel(rows, heads, members, groups, reverse, *refs):
    outs = 2 if heads else 1
    got_ref, *total_refs = refs[:-outs]
    running_ref = refs[-outs]
    group = lax.axis_index("seq") // members
    state = jnp.zeros((rows, HEAD_DIM), F32)
    for step, ref in enumerate(total_refs, 1):
        ahead = group + step < groups if reverse else group >= step
        state += jnp.where(ahead, ref[:rows, :].astype(F32), 0.0)
    order = range(members - 1, -1, -1) if reverse else range(members)
    for member in order:
        running_ref[member] = state.astype(BF16)
        state += got_ref[member, :rows, :].astype(F32)
    if heads:
        gain = gain_sum(rows, heads, got_ref)
        for ref in total_refs:
            both = ref[rows:rows + 2 * heads, :].astype(F32)
            gain += both[:heads] + both[heads:]
        refs[-1][...] = gain


def exclusive_sums(shares, rows, heads, reverse):
    count = lax.axis_size("seq")
    members = shares.shape[0]
    groups = count // members
    index_groups = [list(range(g * members, (g + 1) * members)) for g in range(groups)]
    exchange = functools.partial(
        lax.all_to_all, axis_name="seq", split_axis=0, concat_axis=0, axis_index_groups=index_groups, tiled=True
    )
    got = exchange(shares)
    totals = []
    if groups > 1:
        total = call(
            functools.partial(total_kernel, rows, heads), shape(shares.shape[1:], BF16), got
        )
        for step in range(1, groups):
            hop = (-step if reverse else step) * members
            totals.append(lax.ppermute(total, "seq", [(i, (i + hop) % count) for i in range(count)]))
    outs = [shape((members, rows, HEAD_DIM), BF16)]
    if heads:
        outs.append(shape((heads, HEAD_DIM), F32))
    running, *gain = call(
        functools.partial(running_kernel, rows, heads, members, groups, reverse), outs, got, *totals
    )
    return exchange(running).reshape(members * rows, HEAD_DIM), *gain


def sums_over_heads(sums):
    count = lax.axis_size("head")
    return [sums] + [
        lax.ppermute(sums, "head", [(i, (i + step) % count) for i in range(count)])
        for step in range(1, count)
    ]


def group_size(count):
    members = 1
    while members < 8 and count % (2 * members) == 0:
        members *= 2
    return members


def body(queries, key_vectors, value_vectors, norm_gain, upstream):
    length, width = queries.shape
    heads = width // HEAD_DIM
    total_width = width * lax.axis_size("head")
    members = group_size(lax.axis_size("seq"))
    rows = width // members
    gain = norm_gain.reshape(heads, HEAD_DIM)
    flat16 = shape((length, width), BF16)
    flat32 = shape((length, width), F32)

    state = call(functools.partial(state_kernel, heads), shape((width, HEAD_DIM), BF16), key_vectors, value_vectors)
    (prior,) = exclusive_sums(state.reshape(members, rows, HEAD_DIM), rows, 0, False)
    weights, inner = call(
        functools.partial(weights_kernel, heads),
        [shape((heads, length, length), BF16), flat32],
        queries, key_vectors, value_vectors,
    )
    out, sums = call(
        functools.partial(out_kernel, heads),
        [flat32, shape((2, length, HEAD_DIM), F32)],
        queries, prior, inner, upstream, gain,
    )
    sums = sums_over_heads(sums)
    extra = -(-2 * heads // 16) * 16
    grad, shares = call(
        functools.partial(grad_out_kernel, heads, total_width, members),
        [flat16, shape((members, rows + extra, HEAD_DIM), BF16)],
        out, upstream, gain, queries, *sums,
    )
    later, grad_gain = exclusive_sums(shares, rows, heads, True)
    attended, grad_q, inner_k, inner_v = call(
        functools.partial(inner_grads_kernel, heads, total_width),
        [flat16, flat16, flat32, flat32],
        queries, key_vectors, value_vectors, gain, out, weights, grad, prior, *sums,
    )
    grad_k, grad_v = call(
        functools.partial(last_grads_kernel, heads),
        [flat16, flat16],
        key_vectors, value_vectors, later, inner_k, inner_v,
    )
    return attended, grad_q, grad_k, grad_v, grad_gain.reshape(-1)


def solution(mesh):
    split_both = P("seq", "head")
    in_specs = (split_both, split_both, split_both, P("head"), split_both)
    out_specs = (split_both, split_both, split_both, split_both, P("head"))
    return jax.shard_map(body, mesh=mesh, in_specs=in_specs, out_specs=out_specs, check_vma=False)
```

time: 438 us -> 94.5 us (0.22)
  the two profiles are of different devices: /device:TPU:1 before, /device:TPU:0 now
where the time goes in v1:
time: 94.5 us; the launch traced here: 93.8 us
  blocking collectives  34.7 us (37%)
  local copies, waits for them, and re-layouts  17.5 us (19%)
  Pallas kernels  14.7 us (16%)
  waiting for transfers between devices  13.9 us (15%)
  starting transfers between devices  12.2 us (13%)
    all_to_all x2, blocking collectives, exclusive_sums(): got = exchange(shares)  34.7 us
    unnamed x44, local copies, waits for them, and re-layouts  17.5 us
    pallas_call x10, Pallas kernels, call(): pl.pallas_call(kernel, out_shape=out_shape, in_specs=[whole] * len(args),...  14.7 us
    ppermute x2, waiting for transfers between devices, exclusive_sums(): lax.ppermute(total, 'seq', [(i, (i + hop) % count) for i in range(count)])  9.17 us
    all_to_all x2, starting transfers between devices, exclusive_sums(): return (exchange(running).reshape(members * rows, HEAD_DIM), *gain)  7.76 us
    ppermute x2, starting transfers between devices, exclusive_sums(): lax.ppermute(total, 'seq', [(i, (i + hop) % count) for i in range(count)])  4.36 us
    all_to_all x2, waiting for transfers between devices, exclusive_sums(): return (exchange(running).reshape(members * rows, HEAD_DIM), *gain)  3.39 us
  transfers between devices with their start and end apart: 5, of which 4 were waited for; matrix products, arithmetic and copies ran while one was open for 0% of the time, Pallas kernels for 9%

profile of v1, /device:TPU:0, one launch (start us, length us, event | category | flops | bytes accessed | tf_op | source)
XLA Modules:
  0.0 93.8 jit_solution(7834884980788331460)
XLA Ops:
  1.8 1.1 %copy-done.3 = bf16[128,3072]{1,0:T(8,128)(2,1)S(1)} copy-done((bf16[128,3072]{1,0:T(8,128)(2,1)S(1)}, bf16[128,3072]{1,0:T(8,128)(2,1)}, u32[]{:S(2)}) %copy-start.3) | copy-done | bytes 786456
  3.3 18.2 %all_to_all.20.got_ref.refs_0_ = bf16[8,384,128]{2,1,0:T(8,128)(2,1)S(1)} all-to-all(bf16[8,384,128]{2,1,0:T(8,128)(2,1)S(1)} %bitcast.7), channel_id=1, replica_groups={{0,2,4,6,8,10,12,14},{16,18,20,22,24,26,28,30},{1,3,5,7,9,11,13,15},{17..., dimensions={0} | all-to-all | bytes 1572864 | tf_op jit(solution)/shard_map/all_to_all | solution.py:182
  21.7 2.7 %collective-permute-start = (bf16[384,128]{1,0:T(8,128)(2,1)S(1)}, bf16[384,128]{1,0:T(8,128)(2,1)S(1)}, u32[]{:S(2)}, u32[]{:S(2)}) collective-permute-start(bf16[384,128]{1,0:T(8,128)(2,1)S(1)} %shard_map.93), channel_id=1, source_target_pairs={{0,16},{2,18},{4,20},{6,22},{8,24},{10,26},{12,28},{14,30},{16,0},... | collective-permute-start | bytes 294920 | tf_op jit(solution)/shard_map/ppermute | solution.py:190
  24.3 4.0 %collective-permute-done.refs_1_ = bf16[384,128]{1,0:T(8,128)(2,1)S(1)} collective-permute-done((bf16[384,128]{1,0:T(8,128)(2,1)S(1)}, bf16[384,128]{1,0:T(8,128)(2,1)S(1)}, u32[]{:S(2)}, u32[]{:S(2)}) %collective-permute-start) | collective-permute-done | bytes 98336 | tf_op jit(solution)/shard_map/ppermute | solution.py:190
  29.3 3.5 %all-to-all-start.1 = ((bf16[8,384,128]{2,1,0:T(8,128)(2,1)}), bf16[8,384,128]{2,1,0:T(8,128)(2,1)S(1)}, u32[]{:S(2)}, u32[]{:S(2)}) async-start(bf16[8,384,128]{2,1,0:T(8,128)(2,1)} %copy-done.7), calls=%async_computation.1 | async-start | bytes 1572864 | tf_op jit(solution)/shard_map/all_to_all | solution.py:197
  32.9 3.8 %shard_map.95 = (bf16[24,128,128]{2,1,0:T(8,128)(2,1)S(1)}, f32[128,3072]{1,0:T(8,128)S(1)}) custom-call(bf16[128,3072]{1,0:T(8,128)(2,1)S(1)} %copy-done, bf16[128,3072]{1,0:T(8,128)(2,1)S(1)} %copy-done.2, bf16[128,3072]{1,0:T(8,128)(2,1)S(1)} %copy-done.4), custom_call_target="tpu_custom_call" | custom-call | tf_op jit(solution)/shard_map/pallas_call | solution.py:18
  36.7 1.2 %copy-done.10 = f32[128,3072]{1,0:T(8,128)} copy-done((f32[128,3072]{1,0:T(8,128)}, f32[128,3072]{1,0:T(8,128)S(1)}, u32[]{:S(2)}) %copy-start.10) | copy-done | bytes 1572888
  38.8 3.4 %all-to-all-done.1 = bf16[8,384,128]{2,1,0:T(8,128)(2,1)S(1)} async-done(((bf16[8,384,128]{2,1,0:T(8,128)(2,1)}), bf16[8,384,128]{2,1,0:T(8,128)(2,1)S(1)}, u32[]{:S(2)}, u32[]{:S(2)}) %all-to-all-start.1) | async-done | bytes 786464 | tf_op jit(solution)/shard_map/all_to_all | solution.py:197
  42.2 1.1 %copy-done.8 = bf16[128,3072]{1,0:T(8,128)(2,1)S(1)} copy-done((bf16[128,3072]{1,0:T(8,128)(2,1)S(1)}, bf16[128,3072]{1,0:T(8,128)(2,1)}, u32[]{:S(2)}) %copy-start.8) | copy-done | bytes 786456
  43.3 1.4 %copy-done.11 = f32[128,3072]{1,0:T(8,128)S(1)} copy-done((f32[128,3072]{1,0:T(8,128)S(1)}, f32[128,3072]{1,0:T(8,128)}, u32[]{:S(2)}) %copy-start.11) | copy-done | bytes 1572888
  45.3 1.3 %collective-permute-done.1.refs_5_.refs_9_ = f32[2,128,128]{2,1,0:T(8,128)S(1)} collective-permute-done((f32[2,128,128]{2,1,0:T(8,128)S(1)}, f32[2,128,128]{2,1,0:T(8,128)S(1)}, u32[]{:S(2)}, u32[]{:S(2)}) %collective-permute-start.1) | collective-permute-done | bytes 131104 | tf_op jit(solution)/shard_map/ppermute | solution.py:203
  47.6 16.5 %all_to_all.21.got_ref.refs_0_ = bf16[8,432,128]{2,1,0:T(8,128)(2,1)S(1)} all-to-all(bf16[8,432,128]{2,1,0:T(8,128)(2,1)S(1)} %get-tuple-element.26), channel_id=1, replica_groups={{0,2,4,6,8,10,12,14},{16,18,20,22,24,26,28,30},{1,3,5,7,9,11,13,15},{17..., dimensions={0} | all-to-all | bytes 1769472 | tf_op jit(solution)/shard_map/all_to_all | solution.py:182
  64.2 1.7 %collective-permute-start.2 = (bf16[432,128]{1,0:T(8,128)(2,1)S(1)}, bf16[432,128]{1,0:T(8,128)(2,1)S(1)}, u32[]{:S(2)}, u32[]{:S(2)}) collective-permute-start(bf16[432,128]{1,0:T(8,128)(2,1)S(1)} %shard_map.99), channel_id=1, source_target_pairs={{0,16},{2,18},{4,20},{6,22},{8,24},{10,26},{12,28},{14,30},{16,0},... | collective-permute-start | bytes 331784 | tf_op jit(solution)/shard_map/ppermute | solution.py:190
  65.9 5.2 %collective-permute-done.2.refs_1_ = bf16[432,128]{1,0:T(8,128)(2,1)S(1)} collective-permute-done((bf16[432,128]{1,0:T(8,128)(2,1)S(1)}, bf16[432,128]{1,0:T(8,128)(2,1)S(1)}, u32[]{:S(2)}, u32[]{:S(2)}) %collective-permute-start.2) | collective-permute-done | bytes 110624 | tf_op jit(solution)/shard_map/ppermute | solution.py:190
  72.7 4.2 %all-to-all-start.3 = ((bf16[8,384,128]{2,1,0:T(8,128)(2,1)}), bf16[8,384,128]{2,1,0:T(8,128)(2,1)}, u32[]{:S(2)}, u32[]{:S(2)}) async-start(bf16[8,384,128]{2,1,0:T(8,128)(2,1)} %copy-done.16), calls=%async_computation.3 | async-start | bytes 1572864 | tf_op jit(solution)/shard_map/all_to_all | solution.py:197
  76.9 1.4 %copy-done.6 = f32[128,3072]{1,0:T(8,128)S(1)} copy-done((f32[128,3072]{1,0:T(8,128)S(1)}, f32[128,3072]{1,0:T(8,128)}, u32[]{:S(2)}) %copy-start.6) | copy-done | bytes 1572888
  78.3 1.1 %copy-done.18 = bf16[24,128,128]{2,1,0:T(8,128)(2,1)S(1)} copy-done((bf16[24,128,128]{2,1,0:T(8,128)(2,1)S(1)}, bf16[24,128,128]{2,1,0:T(8,128)(2,1)}, u32[]{:S(2)}) %copy-start.18) | copy-done | bytes 786456
  79.4 1.1 %copy-done.20 = bf16[128,3072]{1,0:T(8,128)(2,1)S(1)} copy-done((bf16[128,3072]{1,0:T(8,128)(2,1)S(1)}, bf16[128,3072]{1,0:T(8,128)(2,1)}, u32[]{:S(2)}) %copy-start.20) | copy-done | bytes 786456
  80.6 4.9 %shard_map.98 = (bf16[128,3072]{1,0:T(8,128)(2,1)}, bf16[128,3072]{1,0:T(8,128)(2,1)}, f32[128,3072]{1,0:T(8,128)S(1)}, f32[128,3072]{1,0:T(8,128)S(1)}) custom-call(bf16[128,3072]{1,0:T(8,128)(2,1)S(1)} %copy-done, bf16[128,3072]{1,0:T(8,128)(2,1)S(1)} %copy-done.2, bf16[128,3072]{1,0:T(8,128)(2,1)S(1)} %copy-done.4, f32[24,128]{1,0:T(8,128)S(1)} %bitcast.10, ...), custom_call_target="tpu_custom_call" | custom-call | tf_op jit(solution)/shard_map/pallas_call | solution.py:18
  85.5 1.2 %copy-done.12 = f32[128,3072]{1,0:T(8,128)} copy-done((f32[128,3072]{1,0:T(8,128)}, f32[128,3072]{1,0:T(8,128)S(1)}, u32[]{:S(2)}) %copy-start.12) | copy-done | bytes 1572888
  86.7 1.2 %copy-done.14 = f32[128,3072]{1,0:T(8,128)} copy-done((f32[128,3072]{1,0:T(8,128)}, f32[128,3072]{1,0:T(8,128)S(1)}, u32[]{:S(2)}) %copy-start.14) | copy-done | bytes 1572888
  87.9 1.4 %copy-done.13 = f32[128,3072]{1,0:T(8,128)S(1)} copy-done((f32[128,3072]{1,0:T(8,128)S(1)}, f32[128,3072]{1,0:T(8,128)}, u32[]{:S(2)}) %copy-start.13) | copy-done | bytes 1572888
  89.3 1.4 %copy-done.15 = f32[128,3072]{1,0:T(8,128)S(1)} copy-done((f32[128,3072]{1,0:T(8,128)S(1)}, f32[128,3072]{1,0:T(8,128)}, u32[]{:S(2)}) %copy-start.15) | copy-done | bytes 1572888
  90.7 3.1 %shard_map.101 = (bf16[128,3072]{1,0:T(8,128)(2,1)}, bf16[128,3072]{1,0:T(8,128)(2,1)}) custom-call(bf16[128,3072]{1,0:T(8,128)(2,1)S(1)} %copy-done.2, bf16[128,3072]{1,0:T(8,128)(2,1)S(1)} %copy-done.4, bf16[3072,128]{1,0:T(8,128)(2,1)} %bitcast.3.later_ref, f32[128,3072]{1,0:T(8,128)S(1)} %copy-done.13, f32[128,3072]{1,0:T(8,128)S(1)} %copy-done.15), custom_call_target="tpu_custom_call" | custom-call | tf_op jit(solution)/shard_map/pallas_call | solution.py:18
  (42 shorter events, 6.8 us)
Async XLA Ops:
  0.6 1.1 %copy-start.1 = (bf16[128,3072]{1,0:T(8,128)(2,1)S(1)}, bf16[128,3072]{1,0:T(8,128)(2,1)}, u32[]{:S(2)}) copy-start(bf16[128,3072]{1,0:T(8,128)(2,1)} %key_ref.5) | copy-start | bytes 2359300
  1.8 1.1 %copy-start.3 = (bf16[128,3072]{1,0:T(8,128)(2,1)S(1)}, bf16[128,3072]{1,0:T(8,128)(2,1)}, u32[]{:S(2)}) copy-start(bf16[128,3072]{1,0:T(8,128)(2,1)} %value_ref.5) | copy-start | bytes 2359300
  21.6 11.3 %copy-start = (bf16[128,3072]{1,0:T(8,128)(2,1)S(1)}, bf16[128,3072]{1,0:T(8,128)(2,1)}, u32[]{:S(2)}) copy-start(bf16[128,3072]{1,0:T(8,128)(2,1)} %refs_0_.1) | copy-start | bytes 2359300
  21.6 11.3 %copy-start.2 = (bf16[128,3072]{1,0:T(8,128)(2,1)S(1)}, bf16[128,3072]{1,0:T(8,128)(2,1)}, u32[]{:S(2)}) copy-start(bf16[128,3072]{1,0:T(8,128)(2,1)} %key_ref.5) | copy-start | bytes 2359300
  21.7 11.3 %copy-start.4 = (bf16[128,3072]{1,0:T(8,128)(2,1)S(1)}, bf16[128,3072]{1,0:T(8,128)(2,1)}, u32[]{:S(2)}) copy-start(bf16[128,3072]{1,0:T(8,128)(2,1)} %value_ref.5) | copy-start | bytes 2359300
  21.7 6.6 %collective-permute-start = (bf16[384,128]{1,0:T(8,128)(2,1)S(1)}, bf16[384,128]{1,0:T(8,128)(2,1)S(1)}, u32[]{:S(2)}, u32[]{:S(2)}) collective-permute-start(bf16[384,128]{1,0:T(8,128)(2,1)S(1)} %shard_map.93), channel_id=1, source_target_pairs={{0,16},{2,18},{4,20},{6,22},{8,24},{10,26},{12,28},{14,30},{16,0},... | collective-permute-start | bytes 294920 | tf_op jit(solution)/shard_map/ppermute | solution.py:190
  29.3 12.8 %all-to-all-start.1 = ((bf16[8,384,128]{2,1,0:T(8,128)(2,1)}), bf16[8,384,128]{2,1,0:T(8,128)(2,1)S(1)}, u32[]{:S(2)}, u32[]{:S(2)}) async-start(bf16[8,384,128]{2,1,0:T(8,128)(2,1)} %copy-done.7), calls=%async_computation.1 | async-start | bytes 1572864 | tf_op jit(solution)/shard_map/all_to_all | solution.py:197
  32.9 9.3 %copy-start.21 = (f32[3072]{0:T(1024)S(1)}, f32[3072]{0:T(1024)}, u32[]{:S(2)}) copy-start(f32[3072]{0:T(1024)} %param.8) | copy-start | bytes 36868
  36.7 1.2 %copy-start.10 = (f32[128,3072]{1,0:T(8,128)}, f32[128,3072]{1,0:T(8,128)S(1)}, u32[]{:S(2)}) copy-start(f32[128,3072]{1,0:T(8,128)S(1)} %get-tuple-element.19.inner_ref) | copy-start | bytes 4718596
  42.2 1.1 %copy-start.8 = (bf16[128,3072]{1,0:T(8,128)(2,1)S(1)}, bf16[128,3072]{1,0:T(8,128)(2,1)}, u32[]{:S(2)}) copy-start(bf16[128,3072]{1,0:T(8,128)(2,1)} %refs_1_.2) | copy-start | bytes 2359300
  43.3 1.4 %copy-start.11 = (f32[128,3072]{1,0:T(8,128)S(1)}, f32[128,3072]{1,0:T(8,128)}, u32[]{:S(2)}) copy-start(f32[128,3072]{1,0:T(8,128)} %copy-done.10) | copy-start | bytes 4718596
  44.7 2.0 %copy-start.9 = (bf16[128,3072]{1,0:T(8,128)(2,1)S(1)}, bf16[128,3072]{1,0:T(8,128)(2,1)}, u32[]{:S(2)}) copy-start(bf16[128,3072]{1,0:T(8,128)(2,1)} %refs_1_.2) | copy-start | bytes 2359300
  45.3 2.3 %copy-start.5 = (f32[128,3072]{1,0:T(8,128)}, f32[128,3072]{1,0:T(8,128)S(1)}, u32[]{:S(2)}) copy-start(f32[128,3072]{1,0:T(8,128)S(1)} %get-tuple-element.20.refs_0_.refs_4_) | copy-start | bytes 4718596
  45.3 1.4 %collective-permute-start.1 = (f32[2,128,128]{2,1,0:T(8,128)S(1)}, f32[2,128,128]{2,1,0:T(8,128)S(1)}, u32[]{:S(2)}, u32[]{:S(2)}) collective-permute-start(f32[2,128,128]{2,1,0:T(8,128)S(1)} %get-tuple-element.22.refs_4_.refs_8_), channel_id=1, source_target_pairs={{0,1},{1,0},{2,3},{3,2},{4,5},{5,4},{6,7},{7,6},{8,9},{9,8},{10,11... | collective-permute-start | bytes 393224 | tf_op jit(solution)/shard_map/ppermute | solution.py:203
  47.6 24.2 %copy-start.19 = (bf16[128,3072]{1,0:T(8,128)(2,1)}, bf16[128,3072]{1,0:T(8,128)(2,1)S(1)}, u32[]{:S(2)}) copy-start(bf16[128,3072]{1,0:T(8,128)(2,1)S(1)} %get-tuple-element.23.refs_6_) | copy-start | bytes 2359300
  64.2 6.9 %collective-permute-start.2 = (bf16[432,128]{1,0:T(8,128)(2,1)S(1)}, bf16[432,128]{1,0:T(8,128)(2,1)S(1)}, u32[]{:S(2)}, u32[]{:S(2)}) collective-permute-start(bf16[432,128]{1,0:T(8,128)(2,1)S(1)} %shard_map.99), channel_id=1, source_target_pairs={{0,16},{2,18},{4,20},{6,22},{8,24},{10,26},{12,28},{14,30},{16,0},... | collective-permute-start | bytes 331784 | tf_op jit(solution)/shard_map/ppermute | solution.py:190
  72.7 15.2 %all-to-all-start.3 = ((bf16[8,384,128]{2,1,0:T(8,128)(2,1)}), bf16[8,384,128]{2,1,0:T(8,128)(2,1)}, u32[]{:S(2)}, u32[]{:S(2)}) async-start(bf16[8,384,128]{2,1,0:T(8,128)(2,1)} %copy-done.16), calls=%async_computation.3 | async-start | bytes 1572864 | tf_op jit(solution)/shard_map/all_to_all | solution.py:197
  76.9 1.4 %copy-start.6 = (f32[128,3072]{1,0:T(8,128)S(1)}, f32[128,3072]{1,0:T(8,128)}, u32[]{:S(2)}) copy-start(f32[128,3072]{1,0:T(8,128)} %copy-done.5) | copy-start | bytes 4718596
  78.3 1.1 %copy-start.18 = (bf16[24,128,128]{2,1,0:T(8,128)(2,1)S(1)}, bf16[24,128,128]{2,1,0:T(8,128)(2,1)}, u32[]{:S(2)}) copy-start(bf16[24,128,128]{2,1,0:T(8,128)(2,1)} %copy-done.17) | copy-start | bytes 2359300
  79.4 1.1 %copy-start.20 = (bf16[128,3072]{1,0:T(8,128)(2,1)S(1)}, bf16[128,3072]{1,0:T(8,128)(2,1)}, u32[]{:S(2)}) copy-start(bf16[128,3072]{1,0:T(8,128)(2,1)} %copy-done.19) | copy-start | bytes 2359300
  85.5 1.2 %copy-start.12 = (f32[128,3072]{1,0:T(8,128)}, f32[128,3072]{1,0:T(8,128)S(1)}, u32[]{:S(2)}) copy-start(f32[128,3072]{1,0:T(8,128)S(1)} %get-tuple-element.28.inner_k_ref) | copy-start | bytes 4718596
  86.7 1.2 %copy-start.14 = (f32[128,3072]{1,0:T(8,128)}, f32[128,3072]{1,0:T(8,128)S(1)}, u32[]{:S(2)}) copy-start(f32[128,3072]{1,0:T(8,128)S(1)} %get-tuple-element.29.inner_v_ref) | copy-start | bytes 4718596
  87.9 1.4 %copy-start.13 = (f32[128,3072]{1,0:T(8,128)S(1)}, f32[128,3072]{1,0:T(8,128)}, u32[]{:S(2)}) copy-start(f32[128,3072]{1,0:T(8,128)} %copy-done.12) | copy-start | bytes 4718596
  89.3 1.4 %copy-start.15 = (f32[128,3072]{1,0:T(8,128)S(1)}, f32[128,3072]{1,0:T(8,128)}, u32[]{:S(2)}) copy-start(f32[128,3072]{1,0:T(8,128)} %copy-done.14) | copy-start | bytes 4718596
  (3 other events, 2.7 us)

commit v2 on v1

v2 whole, which is shorter than its diff:
```python
import functools

import jax
import jax.numpy as jnp
from jax import lax
from jax.experimental import pallas as pl
from jax.experimental.pallas import tpu as pltpu
from jax.sharding import PartitionSpec as P

HEAD_DIM = 128
F32 = jnp.float32
BF16 = jnp.bfloat16
VMEM_LIMIT = 40 * 1024 * 1024
WHOLE = pl.BlockSpec(memory_space=pltpu.VMEM)
FAR = pl.BlockSpec(memory_space=pltpu.HBM)


def shape(dims, dtype):
    return jax.ShapeDtypeStruct(dims, dtype)


def call(kernel, out_shape, *args):
    return pl.pallas_call(
        kernel,
        out_shape=out_shape,
        in_specs=[WHOLE] * len(args),
        out_specs=jax.tree.map(lambda _: WHOLE, out_shape),
        compiler_params=pltpu.CompilerParams(vmem_limit_bytes=VMEM_LIMIT),
    )(*args)


def dot(a, b, over):
    return lax.dot_general(a, b, ((over[:1], over[1:]), ((), ())), preferred_element_type=F32)


def split(value):
    high = value.astype(BF16)
    return high, (value - high.astype(F32)).astype(BF16)


def columns(head):
    return pl.ds(head * HEAD_DIM, HEAD_DIM)


def causal_mask(length):
    rows = lax.broadcasted_iota(jnp.int32, (length, length), 0)
    cols = lax.broadcasted_iota(jnp.int32, (length, length), 1)
    return cols <= rows


def leaving(kernel, heads, ins, outs, near_outs=(), blocks=4):
    while heads % blocks:
        blocks -= 1
    step = heads // blocks
    count = len(outs)

    def whole(*refs):
        in_refs, refs = refs[:len(ins)], refs[len(ins):]
        out_refs, refs = refs[:count], refs[count:]
        near_refs, refs = refs[:len(near_outs)], refs[len(near_outs):]
        buffers, sems = refs[:count], refs[count]
        copies = []

        def done(h):
            if h % step == step - 1:
                span = pl.ds((h + 1 - step) * HEAD_DIM, step * HEAD_DIM)
                for i, (ref, buffer) in enumerate(zip(out_refs, buffers)):
                    copy = pltpu.make_async_copy(buffer.at[:, span], ref.at[:, span], sems.at[h // step, i])
                    copy.start()
                    copies.append(copy)

        kernel(done, *in_refs, *buffers, *near_refs)
        for copy in copies:
            copy.wait()

    return pl.pallas_call(
        whole,
        out_shape=list(outs) + list(near_outs),
        in_specs=[WHOLE] * len(ins),
        out_specs=[FAR] * count + [WHOLE] * len(near_outs),
        scratch_shapes=[pltpu.VMEM(a.shape, a.dtype) for a in outs] + [pltpu.SemaphoreType.DMA((blocks, count))],
        compiler_params=pltpu.CompilerParams(vmem_limit_bytes=VMEM_LIMIT),
    )(*ins)


def state_kernel(heads, key_ref, value_ref, state_ref):
    for h in range(heads):
        part = dot(key_ref[:, columns(h)], value_ref[:, columns(h)], (0, 0))
        state_ref[columns(h), :] = part.astype(BF16)


def weights_kernel(heads, query_ref, key_ref, value_ref, weights_ref, inner_ref):
    mask = causal_mask(query_ref.shape[0])
    for h in range(heads):
        scores = dot(query_ref[:, columns(h)], key_ref[:, columns(h)], (1, 1))
        weights = jnp.where(mask, scores, 0.0).astype(BF16)
        weights_ref[h] = weights
        inner_ref[:, columns(h)] = dot(weights, value_ref[:, columns(h)], (1, 0))


def out_kernel(heads, query_ref, inner_ref, up_ref, prior_ref, gain_ref, out_ref, sums_ref):
    squares = jnp.zeros(sums_ref.shape[1:], F32)
    products = jnp.zeros(sums_ref.shape[1:], F32)
    for h in range(heads):
        out = inner_ref[:, columns(h)] + dot(query_ref[:, columns(h)], prior_ref[columns(h), :], (1, 0))
        out_ref[:, columns(h)] = out
        squares += out * out
        products += up_ref[:, columns(h)].astype(F32) * gain_ref[h][None] * out
    sums_ref[0] = squares
    sums_ref[1] = products


def token_factors(total_width, sums_refs):
    sums = functools.reduce(lambda a, b: a + b, [ref[...] for ref in sums_refs])
    inv = lax.rsqrt(jnp.sum(sums[0], axis=1, keepdims=True) / total_width + 1e-6)
    mean_dot = jnp.sum(sums[1], axis=1, keepdims=True) / total_width * inv
    return inv, mean_dot


def gain_rows(heads, parts):
    return -(-heads // parts)


def grad_out_kernel(heads, total_width, parts, *refs):
    out_ref, up_ref, gain_ref, query_ref, *sums_refs = refs[:-2]
    grad_ref, sent_ref = refs[-2:]
    inv, mean_dot = token_factors(total_width, sums_refs)
    rows = heads * HEAD_DIM // parts
    each = gain_rows(heads, parts)
    sent_ref[:, rows:, :] = jnp.zeros((parts, sent_ref.shape[1] - rows, HEAD_DIM), BF16)
    gains = []
    for h in range(heads):
        scaled = out_ref[:, columns(h)] * inv
        up = up_ref[:, columns(h)].astype(F32)
        grad = (inv * (up * gain_ref[h][None] - scaled * mean_dot)).astype(BF16)
        grad_ref[:, columns(h)] = grad
        state = dot(query_ref[:, columns(h)], grad, (0, 0)).astype(BF16)
        at = 0
        while at < HEAD_DIM:
            part, row = divmod(h * HEAD_DIM + at, rows)
            count = min(HEAD_DIM - at, rows - row)
            sent_ref[part, row:row + count, :] = state[at:at + count]
            at += count
        gains.append(jnp.sum(up * scaled, axis=0, keepdims=True))
        if h % each == each - 1 or h == heads - 1:
            part = h // each
            high, low = split(jnp.concatenate(gains, axis=0))
            sent_ref[part, rows:rows + len(gains), :] = high
            sent_ref[part, rows + each:rows + each + len(gains), :] = low
            gains = []


def inner_grads_kernel(heads, total_width, done, *refs):
    (query_ref, key_ref, value_ref, out_ref, grad_ref, weights_ref, prior_ref, gain_ref, *sums_refs) = refs[:-4]
    attended_ref, grad_q_ref, inner_k_ref, inner_v_ref = refs[-4:]
    inv, _ = token_factors(total_width, sums_refs)
    mask = causal_mask(query_ref.shape[0])
    for h in range(heads):
        cols = columns(h)
        attended_ref[:, cols] = (out_ref[:, cols] * inv * gain_ref[h][None]).astype(BF16)
        grad = grad_ref[:, cols]
        scores = dot(grad, value_ref[:, cols], (1, 1))
        scores = jnp.where(mask, scores, 0.0).astype(BF16)
        grad_q = dot(scores, key_ref[:, cols], (1, 0)) + dot(grad, prior_ref[cols, :], (1, 1))
        grad_q_ref[:, cols] = grad_q.astype(BF16)
        inner_k_ref[:, cols] = dot(scores, query_ref[:, cols], (0, 0))
        inner_v_ref[:, cols] = dot(weights_ref[h], grad, (0, 0))
        done(h)


def last_grads_kernel(heads, parts, done, *refs):
    key_ref, value_ref, inner_k_ref, inner_v_ref, got_ref, grad_k_ref, grad_v_ref, gain_ref = refs
    rows = heads * HEAD_DIM // parts
    each = gain_rows(heads, parts)
    for h in range(heads):
        cols = columns(h)
        pieces, at = [], 0
        while at < HEAD_DIM:
            part, row = divmod(h * HEAD_DIM + at, rows)
            count = min(HEAD_DIM - at, rows - row)
            pieces.append(got_ref[part, row:row + count, :])
            at += count
        later = pieces[0] if len(pieces) == 1 else jnp.concatenate(pieces, axis=0)
        grad_k = inner_k_ref[:, cols] + dot(value_ref[:, cols], later, (1, 1))
        grad_k_ref[:, cols] = grad_k.astype(BF16)
        grad_v = inner_v_ref[:, cols] + dot(key_ref[:, cols], later, (1, 0))
        grad_v_ref[:, cols] = grad_v.astype(BF16)
        done(h)
        part, row = divmod(h, each)
        pair = got_ref[part, rows:rows + 2 * each, :].astype(F32)
        gain_ref[h:h + 1, :] = pair[row:row + 1] + pair[each + row:each + row + 1]


def gain_sum(rows, each, value):
    both = value[rows:rows + 2 * each, :]
    return both[:each] + both[each:]


def store_with_gain(ref, index, state, gain):
    rows, each = state.shape[0], gain.shape[0]
    high, low = split(gain)
    rest = jnp.zeros((ref.shape[-2] - rows - 2 * each, HEAD_DIM), F32)
    tail = jnp.concatenate([high.astype(F32), low.astype(F32), rest], axis=0).astype(BF16)
    ref[index + (slice(0, rows), slice(None))] = state.astype(BF16)
    ref[index + (slice(rows, None), slice(None))] = tail


def total_kernel(rows, each, got_ref, total_ref):
    total = jnp.sum(got_ref[...].astype(F32), axis=0)
    if each:
        store_with_gain(total_ref, (), total[:rows], gain_sum(rows, each, total))
    else:
        total_ref[...] = total.astype(BF16)


def running_kernel(rows, each, members, groups, reverse, *refs):
    got_ref, *total_refs, running_ref = refs
    group = lax.axis_index("seq") // members
    state = jnp.zeros((rows, HEAD_DIM), F32)
    for step, ref in enumerate(total_refs, 1):
        ahead = group + step < groups if reverse else group >= step
        state += jnp.where(ahead, ref[:rows, :].astype(F32), 0.0)
    if each:
        gain = gain_sum(rows, each, jnp.sum(got_ref[...].astype(F32), axis=0))
        for ref in total_refs:
            gain += gain_sum(rows, each, ref[...].astype(F32))
    order = range(members - 1, -1, -1) if reverse else range(members)
    for member in order:
        if each:
            store_with_gain(running_ref, (member,), state, gain)
        else:
            running_ref[member] = state.astype(BF16)
        state += got_ref[member, :rows, :].astype(F32)


def exclusive_sums(shares, rows, each, reverse, beside):
    count = lax.axis_size("seq")
    members = shares.shape[0]
    groups = count // members
    index_groups = [list(range(g * members, (g + 1) * members)) for g in range(groups)]
    exchange = functools.partial(
        lax.all_to_all, axis_name="seq", split_axis=0, concat_axis=0, axis_index_groups=index_groups, tiled=True
    )
    got = exchange(shares)
    totals = []
    if groups > 1:
        total = call(
            functools.partial(total_kernel, rows, each), shape(shares.shape[1:], BF16), got
        )
        for step in range(1, groups):
            hop = (-step if reverse else step) * members
            totals.append(lax.ppermute(total, "seq", [(i, (i + hop) % count) for i in range(count)]))
        got, work = beside(got, total)
    else:
        got, work = beside(got, got)
    running = call(
        functools.partial(running_kernel, rows, each, members, groups, reverse),
        shape(shares.shape, BF16), got, *totals,
    )
    return exchange(running), work


def sums_over_heads(sums):
    count = lax.axis_size("head")
    return [sums] + [
        lax.ppermute(sums, "head", [(i, (i + step) % count) for i in range(count)])
        for step in range(1, count)
    ]


def group_size(count):
    members = 1
    while members < 8 and count % (2 * members) == 0:
        members *= 2
    return members


def tied(value, after):
    return lax.optimization_barrier((value, after))[0]


def body(queries, key_vectors, value_vectors, norm_gain, upstream):
    length, width = queries.shape
    heads = width // HEAD_DIM
    total_width = width * lax.axis_size("head")
    members = group_size(lax.axis_size("seq"))
    rows = width // members
    gain = norm_gain.reshape(heads, HEAD_DIM)
    flat16 = shape((length, width), BF16)
    flat32 = shape((length, width), F32)

    state = call(functools.partial(state_kernel, heads), shape((width, HEAD_DIM), BF16), key_vectors, value_vectors)

    def inner_out(got, total):
        weights, inner = call(
            functools.partial(weights_kernel, heads),
            [shape((heads, length, length), BF16), flat32],
            tied(queries, total), key_vectors, value_vectors,
        )
        return tied(got, inner), (weights, inner)

    prior, (weights, inner) = exclusive_sums(state.reshape(members, rows, HEAD_DIM), rows, 0, False, inner_out)
    prior = prior.reshape(width, HEAD_DIM)
    out, sums = call(
        functools.partial(out_kernel, heads),
        [flat32, shape((2, length, HEAD_DIM), F32)],
        queries, inner, upstream, prior, gain,
    )
    sums = sums_over_heads(sums)
    each = gain_rows(heads, members)
    extra = -(-2 * each // 16) * 16
    grad, shares = call(
        functools.partial(grad_out_kernel, heads, total_width, members),
        [flat16, shape((members, rows + extra, HEAD_DIM), BF16)],
        out, upstream, gain, queries, *sums,
    )

    def inner_grads(got, total):
        attended, grad_q, inner_k, inner_v = leaving(
            functools.partial(inner_grads_kernel, heads, total_width), heads,
            [tied(queries, total), key_vectors, value_vectors, out, grad, weights, prior, gain, *sums],
            [flat16, flat16], [flat32, flat32],
        )
        return tied(got, inner_v), (attended, grad_q, inner_k, inner_v)

    later, (attended, grad_q, inner_k, inner_v) = exclusive_sums(shares, rows, each, True, inner_grads)
    grad_k, grad_v, grad_gain = leaving(
        functools.partial(last_grads_kernel, heads, members), heads,
        [key_vectors, value_vectors, inner_k, inner_v, later],
        [flat16, flat16], [shape((heads, HEAD_DIM), F32)],
    )
    return attended, grad_q, grad_k, grad_v, grad_gain.reshape(-1)


def solution(mesh):
    split_both = P("seq", "head")
    in_specs = (split_both, split_both, split_both, P("head"), split_both)
    out_specs = (split_both, split_both, split_both, split_both, P("head"))
    return jax.shard_map(body, mesh=mesh, in_specs=in_specs, out_specs=out_specs, check_vma=False)
```

time: 94.5 us -> 85.8 us (0.908)
  blocking collectives: 34.7 us -> 62.5 us
  local copies, waits for them, and re-layouts: 17.5 us -> 2.29 us
  waiting for transfers between devices: 13.9 us -> 2.08 us
  starting transfers between devices: 12.2 us -> 4.22 us
  Pallas kernels: 14.7 us -> 13.6 us
    all_to_all x0 -> x2, blocking collectives: none -> 28.3 us  [exclusive_sums(): return (exchange(running), work)]
    unnamed x44 -> x14, local copies, waits for them, and re-layouts: 17.5 us -> 2.29 us
    ppermute x2, waiting for transfers between devices: 9.17 us -> 0.75 us  [exclusive_sums(): lax.ppermute(total, 'seq', [(i, (i + hop) % count) for i in range(count)])]
    all_to_all x2 -> x0, starting transfers between devices: 7.76 us -> none  [exclusive_sums(): return (exchange(running).reshape(members * rows, HEAD_DIM), *gain)]
    all_to_all x2 -> x0, waiting for transfers between devices: 3.39 us -> none  [exclusive_sums(): return (exchange(running).reshape(members * rows, HEAD_DIM), *gain)]
    pallas_call x10, Pallas kernels: 14.7 us -> 13.6 us  [the longest x2 7.36 us: leaving(): pl.pallas_call(whole, out_shape=list(outs) + list(near_outs), in_specs=[W...]
  transfers between devices with their start and end apart: 5 -> 3, of which waited for: 4 -> 3; matrix products, arithmetic and copies ran while one was open for 0% -> 0% of each run, Pallas kernels for 9% -> 10%
where the time goes in v2:
time: 85.8 us; the launch traced here: 85.4 us
  blocking collectives  62.5 us (73%)
  Pallas kernels  13.6 us (16%)
  starting transfers between devices  4.22 us (5%)
  local copies, waits for them, and re-layouts  2.29 us (3%)
  waiting for transfers between devices  2.08 us (2%)
    all_to_all x2, blocking collectives, exclusive_sums(): got = exchange(shares)  34.2 us
    all_to_all x2, blocking collectives, exclusive_sums(): return (exchange(running), work)  28.3 us
    pallas_call x2, Pallas kernels, leaving(): pl.pallas_call(whole, out_shape=list(outs) + list(near_outs), in_specs=[W...  7.36 us
    pallas_call x8, Pallas kernels, call(): pl.pallas_call(kernel, out_shape=out_shape, in_specs=[WHOLE] * len(args),...  6.25 us
    ppermute x2, starting transfers between devices, exclusive_sums(): lax.ppermute(total, 'seq', [(i, (i + hop) % count) for i in range(count)])  4.15 us
    unnamed x14, local copies, waits for them, and re-layouts  2.29 us
  transfers between devices with their start and end apart: 3, of which 3 were waited for; matrix products, arithmetic and copies ran while one was open for 0% of the time, Pallas kernels for 10%

profile of v2, /device:TPU:0, one launch (start us, length us, event | category | flops | bytes accessed | tf_op | source)
XLA Modules:
  0.0 85.4 jit_solution(10905351397530602069)
XLA Ops:
  0.6 0.0 copy-start.1
  0.6 1.1 %copy-done.1 = bf16[128,3072]{1,0:T(8,128)(2,1)S(1)} copy-done((bf16[128,3072]{1,0:T(8,128)(2,1)S(1)}, bf16[128,3072]{1,0:T(8,128)(2,1)}, u32[]{:S(2)}) %copy-start.1) | copy-done | bytes 786456
  1.8 1.1 %copy-done.3 = bf16[128,3072]{1,0:T(8,128)(2,1)S(1)} copy-done((bf16[128,3072]{1,0:T(8,128)(2,1)S(1)}, bf16[128,3072]{1,0:T(8,128)(2,1)}, u32[]{:S(2)}) %copy-start.3) | copy-done | bytes 786456
  2.9 0.4 shard_map.92
  3.3 0.0 copy-start
  3.4 18.3 %all_to_all.20.got_ref.refs_0_ = bf16[8,384,128]{2,1,0:T(8,128)(2,1)S(1)} all-to-all(bf16[8,384,128]{2,1,0:T(8,128)(2,1)S(1)} %bitcast.6), channel_id=1, replica_groups={{0,2,4,6,8,10,12,14},{16,18,20,22,24,26,28,30},{1,3,5,7,9,11,13,15},{17..., dimensions={0} | all-to-all | bytes 1572864 | tf_op jit(solution)/shard_map/all_to_all | solution.py:244
  21.7 0.1 shard_map.93
  21.8 2.7 %collective-permute-start = (bf16[384,128]{1,0:T(8,128)(2,1)S(1)}, bf16[384,128]{1,0:T(8,128)(2,1)S(1)}, u32[]{:S(2)}, u32[]{:S(2)}) collective-permute-start(bf16[384,128]{1,0:T(8,128)(2,1)S(1)} %shard_map.93), channel_id=1, source_target_pairs={{0,16},{2,18},{4,20},{6,22},{8,24},{10,26},{12,28},{14,30},{16,0},... | collective-permute-start | bytes 294920 | tf_op jit(solution)/shard_map/ppermute | solution.py:252
  24.5 3.8 %shard_map.94 = (bf16[24,128,128]{2,1,0:T(8,128)(2,1)S(1)}, f32[128,3072]{1,0:T(8,128)S(1)}) custom-call(bf16[128,3072]{1,0:T(8,128)(2,1)S(1)} %copy-done, bf16[128,3072]{1,0:T(8,128)(2,1)S(1)} %copy-done.2, bf16[128,3072]{1,0:T(8,128)(2,1)S(1)} %copy-done.4), custom_call_target="tpu_custom_call" | custom-call | tf_op jit(solution)/shard_map/pallas_call | solution.py:23
  28.3 0.1 collective-permute-done.refs_1_
  28.4 0.1 shard_map.95
  28.6 13.1 %all_to_all.21 = bf16[8,384,128]{2,1,0:T(8,128)(2,1)S(1)} all-to-all(bf16[8,384,128]{2,1,0:T(8,128)(2,1)S(1)} %shard_map.95), channel_id=1, replica_groups={{0,2,4,6,8,10,12,14},{16,18,20,22,24,26,28,30},{1,3,5,7,9,11,13,15},{17..., dimensions={0} | all-to-all | bytes 1572864 | tf_op jit(solution)/shard_map/all_to_all | solution.py:260
  41.7 0.6 shard_map.96
  42.3 0.1 collective-permute-start.1
  42.4 1.3 %collective-permute-done.1.refs_5_.refs_9_ = f32[2,128,128]{2,1,0:T(8,128)S(1)} collective-permute-done((f32[2,128,128]{2,1,0:T(8,128)S(1)}, f32[2,128,128]{2,1,0:T(8,128)S(1)}, u32[]{:S(2)}, u32[]{:S(2)}) %collective-permute-start.1) | collective-permute-done | bytes 131104 | tf_op jit(solution)/shard_map/ppermute | solution.py:266
  43.7 1.0 %shard_map.97 = (bf16[128,3072]{1,0:T(8,128)(2,1)S(1)}, bf16[8,400,128]{2,1,0:T(8,128)(2,1)S(1)}) custom-call(f32[128,3072]{1,0:T(8,128)S(1)} %get-tuple-element.25.refs_0_.refs_3_, bf16[128,3072]{1,0:T(8,128)(2,1)S(1)} %copy-done.5, f32[24,128]{1,0:T(8,128)S(1)} %bitcast.8, bf16[128,3072]{1,0:T(8,128)(2,1)S(1)} %copy-done, ...), custom_call_target="tpu_custom_call" | custom-call | tf_op jit(solution)/shard_map/pallas_call | solution.py:23
  44.7 15.9 %all_to_all.22.got_ref.refs_0_ = bf16[8,400,128]{2,1,0:T(8,128)(2,1)S(1)} all-to-all(bf16[8,400,128]{2,1,0:T(8,128)(2,1)S(1)} %get-tuple-element.27), channel_id=1, replica_groups={{0,2,4,6,8,10,12,14},{16,18,20,22,24,26,28,30},{1,3,5,7,9,11,13,15},{17..., dimensions={0} | all-to-all | bytes 1638400 | tf_op jit(solution)/shard_map/all_to_all | solution.py:244
  60.5 0.1 shard_map.98
  60.6 1.5 %collective-permute-start.2 = (bf16[400,128]{1,0:T(8,128)(2,1)S(1)}, bf16[400,128]{1,0:T(8,128)(2,1)S(1)}, u32[]{:S(2)}, u32[]{:S(2)}) collective-permute-start(bf16[400,128]{1,0:T(8,128)(2,1)S(1)} %shard_map.98), channel_id=1, source_target_pairs={{0,16},{2,18},{4,20},{6,22},{8,24},{10,26},{12,28},{14,30},{16,0},... | collective-permute-start | bytes 307208 | tf_op jit(solution)/shard_map/ppermute | solution.py:252
  62.1 5.1 %shard_map.99 = (bf16[128,3072]{1,0:T(8,128)(2,1)}, bf16[128,3072]{1,0:T(8,128)(2,1)}, f32[128,3072]{1,0:T(8,128)S(1)}, f32[128,3072]{1,0:T(8,128)S(1)}) custom-call(bf16[128,3072]{1,0:T(8,128)(2,1)S(1)} %copy-done, bf16[128,3072]{1,0:T(8,128)(2,1)S(1)} %copy-done.2, bf16[128,3072]{1,0:T(8,128)(2,1)S(1)} %copy-done.4, ...), custom_call_target="tpu_custom_call" | custom-call | tf_op jit(solution)/shard_map/pallas_call | solution.py:76
  67.2 0.6 collective-permute-done.2.refs_1_
  67.8 0.2 shard_map.100
  68.0 15.2 %all_to_all.23.refs_4_ = bf16[8,400,128]{2,1,0:T(8,128)(2,1)S(1)} all-to-all(bf16[8,400,128]{2,1,0:T(8,128)(2,1)S(1)} %shard_map.100), channel_id=1, replica_groups={{0,2,4,6,8,10,12,14},{16,18,20,22,24,26,28,30},{1,3,5,7,9,11,13,15},{17..., dimensions={0} | all-to-all | bytes 1638400 | tf_op jit(solution)/shard_map/all_to_all | solution.py:260
  83.2 2.2 %shard_map.101 = (bf16[128,3072]{1,0:T(8,128)(2,1)}, bf16[128,3072]{1,0:T(8,128)(2,1)}, f32[24,128]{1,0:T(8,128)}) custom-call(bf16[128,3072]{1,0:T(8,128)(2,1)S(1)} %copy-done.2, bf16[128,3072]{1,0:T(8,128)(2,1)S(1)} %copy-done.4, f32[128,3072]{1,0:T(8,128)S(1)} %get-tuple-element.33.refs_2_, f32[128,3072]{1,0:T(8,128)S(1)} %get-tuple-element.34.refs_3_, ...), custom_call_target="tpu_custom_call" | custom-call | tf_op jit(solution)/shard_map/pallas_call | solution.py:76
  (10 shorter events, 0.0 us)
Async XLA Ops:
  0.6 1.1 %copy-start.1 = (bf16[128,3072]{1,0:T(8,128)(2,1)S(1)}, bf16[128,3072]{1,0:T(8,128)(2,1)}, u32[]{:S(2)}) copy-start(bf16[128,3072]{1,0:T(8,128)(2,1)} %refs_0_.2) | copy-start | bytes 2359300
  1.8 1.1 %copy-start.3 = (bf16[128,3072]{1,0:T(8,128)(2,1)S(1)}, bf16[128,3072]{1,0:T(8,128)(2,1)}, u32[]{:S(2)}) copy-start(bf16[128,3072]{1,0:T(8,128)(2,1)} %refs_1_.5) | copy-start | bytes 2359300
  3.3 21.1 %copy-start = (bf16[128,3072]{1,0:T(8,128)(2,1)S(1)}, bf16[128,3072]{1,0:T(8,128)(2,1)}, u32[]{:S(2)}) copy-start(bf16[128,3072]{1,0:T(8,128)(2,1)} %refs_0_.1) | copy-start | bytes 2359300
  3.3 21.1 %copy-start.2 = (bf16[128,3072]{1,0:T(8,128)(2,1)S(1)}, bf16[128,3072]{1,0:T(8,128)(2,1)}, u32[]{:S(2)}) copy-start(bf16[128,3072]{1,0:T(8,128)(2,1)} %refs_0_.2) | copy-start | bytes 2359300
  3.3 21.1 %copy-start.4 = (bf16[128,3072]{1,0:T(8,128)(2,1)S(1)}, bf16[128,3072]{1,0:T(8,128)(2,1)}, u32[]{:S(2)}) copy-start(bf16[128,3072]{1,0:T(8,128)(2,1)} %refs_1_.5) | copy-start | bytes 2359300
  21.8 6.6 %collective-permute-start = (bf16[384,128]{1,0:T(8,128)(2,1)S(1)}, bf16[384,128]{1,0:T(8,128)(2,1)S(1)}, u32[]{:S(2)}, u32[]{:S(2)}) collective-permute-start(bf16[384,128]{1,0:T(8,128)(2,1)S(1)} %shard_map.93), channel_id=1, source_target_pairs={{0,16},{2,18},{4,20},{6,22},{8,24},{10,26},{12,28},{14,30},{16,0},... | collective-permute-start | bytes 294920 | tf_op jit(solution)/shard_map/ppermute | solution.py:252
  28.3 13.4 %copy-start.5 = (bf16[128,3072]{1,0:T(8,128)(2,1)S(1)}, bf16[128,3072]{1,0:T(8,128)(2,1)}, u32[]{:S(2)}) copy-start(bf16[128,3072]{1,0:T(8,128)(2,1)} %refs_1_.3) | copy-start | bytes 2359300
  28.3 13.4 %copy-start.6 = (f32[3072]{0:T(1024)S(1)}, f32[3072]{0:T(1024)}, u32[]{:S(2)}) copy-start(f32[3072]{0:T(1024)} %param.8) | copy-start | bytes 36868
  42.3 1.4 %collective-permute-start.1 = (f32[2,128,128]{2,1,0:T(8,128)S(1)}, f32[2,128,128]{2,1,0:T(8,128)S(1)}, u32[]{:S(2)}, u32[]{:S(2)}) collective-permute-start(f32[2,128,128]{2,1,0:T(8,128)S(1)} %get-tuple-element.26.refs_4_.refs_8_), channel_id=1, source_target_pairs={{0,1},{1,0},{2,3},{3,2},{4,5},{5,4},{6,7},{7,6},{8,9},{9,8},{10,11... | collective-permute-start | bytes 393224 | tf_op jit(solution)/shard_map/ppermute | solution.py:266
  60.6 7.2 %collective-permute-start.2 = (bf16[400,128]{1,0:T(8,128)(2,1)S(1)}, bf16[400,128]{1,0:T(8,128)(2,1)S(1)}, u32[]{:S(2)}, u32[]{:S(2)}) collective-permute-start(bf16[400,128]{1,0:T(8,128)(2,1)S(1)} %shard_map.98), channel_id=1, source_target_pairs={{0,16},{2,18},{4,20},{6,22},{8,24},{10,26},{12,28},{14,30},{16,0},... | collective-permute-start | bytes 307208 | tf_op jit(solution)/shard_map/ppermute | solution.py:252

commit v3 on v2

--- a/solution.py
+++ b/solution.py
@@ -48,54 +48,111 @@
     return cols <= rows
 
 
-def leaving(kernel, heads, ins, outs, near_outs=(), blocks=4):
+def first_core(mine, other):
+    odd = lax.axis_index("head") % 2
+    pl.when(odd == 0)(mine)
+    pl.when(odd == 1)(other)
+
+
+def leave(kernel, span, ins, outs, buffers, sems, blocks):
+    if not span:
+        return
+    step = -(-len(span) // blocks)
+    copies = []
+
+    def done(h):
+        place = h - span.start
+        if place % step == step - 1 or h == span[-1]:
+            first = span.start + place // step * step
+            cols = pl.ds(first * HEAD_DIM, (h + 1 - first) * HEAD_DIM)
+            for i, (out, buffer) in enumerate(zip(outs, buffers)):
+                copy = pltpu.make_async_copy(buffer.at[:, cols], out.at[:, cols], sems.at[place // step, i])
+                copy.start()
+                copies.append(copy)
+
+    kernel(span, done, *ins, *buffers)
+    for copy in copies:
+        copy.wait()
+
+
+def leaving(kernel, spans, ins, outs, near_outs=(), held=(), blocks=4):
+    count = len(outs)
+
+    def whole(*refs):
+        in_refs, refs = refs[:len(ins)], refs[len(ins) + len(held):]
+        out_refs, refs = refs[:count], refs[count:]
+        near_refs, refs = refs[:len(near_outs)], refs[len(near_outs):]
+        buffers, sems = refs[:count], refs[count]
+        work = lambda span: leave(kernel, span, in_refs + near_refs, out_refs, buffers, sems, blocks)
+        if spans[0] == spans[1]:
+            work(spans[0])
+        else:
+            first_core(lambda: work(spans[0]), lambda: work(spans[1]))
+
+    return pl.pallas_call(
+        whole,
+        out_shape=list(outs) + list(near_outs),
+        in_specs=[WHOLE] * len(ins) + [FAR] * len(held),
+        out_specs=[FAR] * count + [WHOLE] * len(near_outs),
+        scratch_shapes=[pltpu.VMEM(a.shape, a.dtype) for a in outs] + [pltpu.SemaphoreType.DMA((blocks, count))],
+        input_output_aliases={len(ins) + i: i for i in range(len(held))},
+        compiler_params=pltpu.CompilerParams(vmem_limit_bytes=VMEM_LIMIT),
+    )(*ins, *held)
+
+
+def inner_out_kernel(span, done, query_ref, key_ref, value_ref, weights_ref, inner_ref):
+    mask = causal_mask(query_ref.shape[0])
+    for h in span:
+        cols = columns(h)
+        scores = dot(query_ref[:, cols], key_ref[:, cols], (1, 1))
+        weights = jnp.where(mask, scores, 0.0).astype(BF16)
+        weights_ref[:, cols] = weights
+        inner_ref[:, cols] = dot(weights, value_ref[:, cols], (1, 0))
+        done(h)
+
+
+def local_states(heads, early, queries, key_vectors, value_vectors, outs, blocks=2):
+    length, width = key_vectors.shape
     while heads % blocks:
         blocks -= 1
     step = heads // blocks
-    count = len(outs)
+    sources = [pltpu.with_memory_space_constraint(a, pltpu.HBM) for a in (key_vectors, value_vectors, queries)]
 
     def whole(*refs):
-        in_refs, refs = refs[:len(ins)], refs[len(ins):]
-        out_refs, refs = refs[:count], refs[count:]
-        near_refs, refs = refs[:len(near_outs)], refs[len(near_outs):]
-        buffers, sems = refs[:count], refs[count]
-        copies = []
-
-        def done(h):
-            if h % step == step - 1:
-                span = pl.ds((h + 1 - step) * HEAD_DIM, step * HEAD_DIM)
-                for i, (ref, buffer) in enumerate(zip(out_refs, buffers)):
-                    copy = pltpu.make_async_copy(buffer.at[:, span], ref.at[:, span], sems.at[h // step, i])
-                    copy.start()
-                    copies.append(copy)
-
-        kernel(done, *in_refs, *buffers, *near_refs)
-        for copy in copies:
-            copy.wait()
+        far, (state_ref, *out_refs) = refs[:3], refs[3:6]
+        key_ref, value_ref, query_ref, weights_ref, inner_ref, in_sems, out_sems = refs[6:]
+        arrivals = []
+        for block in range(blocks):
+            cols = pl.ds(block * step * HEAD_DIM, step * HEAD_DIM)
+            for i, (ref, buffer) in enumerate(((far[0], key_ref), (far[1], value_ref))):
+                arrivals.append(pltpu.make_async_copy(ref.at[:, cols], buffer.at[:, cols], in_sems.at[i, block]))
+        cols = pl.ds(0, max(len(early), 1) * HEAD_DIM)
+        query_copy = pltpu.make_async_copy(far[2].at[:, cols], query_ref.at[:, cols], in_sems.at[2, 0])
+        for copy in arrivals:
+            copy.start()
+        query_copy.start()
+        for h in range(heads):
+            if h % step == 0:
+                for copy in arrivals[2 * (h // step):2 * (h // step) + 2]:
+                    copy.wait()
+            part = dot(key_ref[:, columns(h)], value_ref[:, columns(h)], (0, 0))
+            state_ref[columns(h), :] = part.astype(BF16)
+        query_copy.wait()
+        ins = query_ref, key_ref, value_ref
+        first_core(
+            lambda: leave(inner_out_kernel, early, ins, out_refs, (weights_ref, inner_ref), out_sems, 1),
+            lambda: None,
+        )
 
     return pl.pallas_call(
         whole,
-        out_shape=list(outs) + list(near_outs),
-        in_specs=[WHOLE] * len(ins),
-        out_specs=[FAR] * count + [WHOLE] * len(near_outs),
-        scratch_shapes=[pltpu.VMEM(a.shape, a.dtype) for a in outs] + [pltpu.SemaphoreType.DMA((blocks, count))],
+        out_shape=[shape((width, HEAD_DIM), BF16)] + outs,
+        in_specs=[FAR] * 3,
+        out_specs=[WHOLE, FAR, FAR],
+        scratch_shapes=[pltpu.VMEM((length, width), BF16)] * 3 + [pltpu.VMEM(a.shape, a.dtype) for a in outs]
+        + [pltpu.SemaphoreType.DMA((3, blocks)), pltpu.SemaphoreType.DMA((1, 2))],
         compiler_params=pltpu.CompilerParams(vmem_limit_bytes=VMEM_LIMIT),
-    )(*ins)
-
-
-def state_kernel(heads, key_ref, value_ref, state_ref):
-    for h in range(heads):
-        part = dot(key_ref[:, columns(h)], value_ref[:, columns(h)], (0, 0))
-        state_ref[columns(h), :] = part.astype(BF16)
-
-
-def weights_kernel(heads, query_ref, key_ref, value_ref, weights_ref, inner_ref):
-    mask = causal_mask(query_ref.shape[0])
-    for h in range(heads):
-        scores = dot(query_ref[:, columns(h)], key_ref[:, columns(h)], (1, 1))
-        weights = jnp.where(mask, scores, 0.0).astype(BF16)
-        weights_ref[h] = weights
-        inner_ref[:, columns(h)] = dot(weights, value_ref[:, columns(h)], (1, 0))
+    )(*sources)
 
 
 def out_kernel(heads, query_ref, inner_ref, up_ref, prior_ref, gain_ref, out_ref, sums_ref):
@@ -150,29 +207,38 @@
             gains = []
 
 
-def inner_grads_kernel(heads, total_width, done, *refs):
-    (query_ref, key_ref, value_ref, out_ref, grad_ref, weights_ref, prior_ref, gain_ref, *sums_refs) = refs[:-4]
-    attended_ref, grad_q_ref, inner_k_ref, inner_v_ref = refs[-4:]
-    inv, _ = token_factors(total_width, sums_refs)
+def inner_grads_kernel(span, done, *refs):
+    query_ref, value_ref, grad_ref, weights_ref, scores_ref, inner_k_ref, inner_v_ref = refs
     mask = causal_mask(query_ref.shape[0])
-    for h in range(heads):
+    for h in span:
         cols = columns(h)
-        attended_ref[:, cols] = (out_ref[:, cols] * inv * gain_ref[h][None]).astype(BF16)
         grad = grad_ref[:, cols]
         scores = dot(grad, value_ref[:, cols], (1, 1))
         scores = jnp.where(mask, scores, 0.0).astype(BF16)
-        grad_q = dot(scores, key_ref[:, cols], (1, 0)) + dot(grad, prior_ref[cols, :], (1, 1))
+        scores_ref[:, cols] = scores
+        inner_k_ref[:, cols] = dot(scores, query_ref[:, cols], (0, 0))
+        inner_v_ref[:, cols] = dot(weights_ref[:, cols], grad, (0, 0))
+        done(h)
+
+
+def query_grads_kernel(total_width, span, done, *refs):
+    scores_ref, key_ref, grad_ref, prior_ref, out_ref, gain_ref, *sums_refs = refs[:-2]
+    attended_ref, grad_q_ref = refs[-2:]
+    inv, _ = token_factors(total_width, sums_refs)
+    for h in span:
+        cols = columns(h)
+        attended_ref[:, cols] = (out_ref[:, cols] * inv * gain_ref[h][None]).astype(BF16)
+        grad_q = dot(scores_ref[:, cols], key_ref[:, cols], (1, 0)) + dot(grad_ref[:, cols], prior_ref[cols, :], (1, 1))
         grad_q_ref[:, cols] = grad_q.astype(BF16)
-        inner_k_ref[:, cols] = dot(scores, query_ref[:, cols], (0, 0))
-        inner_v_ref[:, cols] = dot(weights_ref[h], grad, (0, 0))
         done(h)
 
 
-def last_grads_kernel(heads, parts, done, *refs):
-    key_ref, value_ref, inner_k_ref, inner_v_ref, got_ref, grad_k_ref, grad_v_ref, gain_ref = refs
+def last_grads_kernel(parts, span, done, *refs):
+    key_ref, value_ref, inner_k_ref, inner_v_ref, got_ref, gain_ref, grad_k_ref, grad_v_ref = refs
+    heads = len(span)
     rows = heads * HEAD_DIM // parts
     each = gain_rows(heads, parts)
-    for h in range(heads):
+    for h in span:
         cols = columns(h)
         pieces, at = [], 0
         while at < HEAD_DIM:
@@ -224,8 +290,9 @@
         gain = gain_sum(rows, each, jnp.sum(got_ref[...].astype(F32), axis=0))
         for ref in total_refs:
             gain += gain_sum(rows, each, ref[...].astype(F32))
-    order = range(members - 1, -1, -1) if reverse else range(members)
-    for member in order:
+    order = member_order(members)
+    for block in range(members - 1, -1, -1) if reverse else range(members):
+        member = order.index(block)
         if each:
             store_with_gain(running_ref, (member,), state, gain)
         else:
@@ -233,11 +300,16 @@
         state += got_ref[member, :rows, :].astype(F32)
 
 
+def member_order(members):
+    quick = (3, 2, 6, 4, 1, 0, 7, 5)
+    return list(quick if len(quick) == members else range(members))
+
+
 def exclusive_sums(shares, rows, each, reverse, beside):
     count = lax.axis_size("seq")
     members = shares.shape[0]
     groups = count // members
-    index_groups = [list(range(g * members, (g + 1) * members)) for g in range(groups)]
+    index_groups = [[g * members + block for block in member_order(members)] for g in range(groups)]
     exchange = functools.partial(
         lax.all_to_all, axis_name="seq", split_axis=0, concat_axis=0, axis_index_groups=index_groups, tiled=True
     )
@@ -288,14 +360,15 @@
     gain = norm_gain.reshape(heads, HEAD_DIM)
     flat16 = shape((length, width), BF16)
     flat32 = shape((length, width), F32)
-
-    state = call(functools.partial(state_kernel, heads), shape((width, HEAD_DIM), BF16), key_vectors, value_vectors)
+    flat_scores = shape((length, heads * length), BF16)
+
+    every, none, early = range(heads), range(0), range(heads // 2)
+    state, *held = local_states(heads, early, queries, key_vectors, value_vectors, [flat_scores, flat32])
 
     def inner_out(got, total):
-        weights, inner = call(
-            functools.partial(weights_kernel, heads),
-            [shape((heads, length, length), BF16), flat32],
-            tied(queries, total), key_vectors, value_vectors,
+        weights, inner = leaving(
+            inner_out_kernel, (every[len(early):], every),
+            [tied(queries, total), key_vectors, value_vectors], [flat_scores, flat32], (), held,
         )
         return tied(got, inner), (weights, inner)
 
@@ -315,17 +388,30 @@
         out, upstream, gain, queries, *sums,
     )
 
-    def inner_grads(got, total):
-        attended, grad_q, inner_k, inner_v = leaving(
-            functools.partial(inner_grads_kernel, heads, total_width), heads,
-            [tied(queries, total), key_vectors, value_vectors, out, grad, weights, prior, gain, *sums],
-            [flat16, flat16], [flat32, flat32],
+    def inner_grads(spans, after, held=(), blocks=4):
+        return leaving(
+            inner_grads_kernel, spans, [tied(queries, after), value_vectors, grad, weights],
+            [flat_scores, flat32, flat32], (), held, blocks,
         )
-        return tied(got, inner_v), (attended, grad_q, inner_k, inner_v)
-
-    later, (attended, grad_q, inner_k, inner_v) = exclusive_sums(shares, rows, each, True, inner_grads)
+
+    def query_grads(spans, after, scores, held=(), blocks=4):
+        return leaving(
+            functools.partial(query_grads_kernel, total_width), spans,
+            [scores, key_vectors, tied(grad, after), prior, out, gain, *sums], [flat16, flat16], (), held, blocks,
+        )
+
+    first = inner_grads((none, every), shares)
+    ready = query_grads((none, every), first, first[0], (), 1)
+    shares = tied(shares, ready)
+
+    def grads_beside(got, total):
+        late = inner_grads((every, none), total, first)
+        results = query_grads((every, none), late, late[0], ready)
+        return tied(got, results), (late, results)
+
+    later, ((_, inner_k, inner_v), (attended, grad_q)) = exclusive_sums(shares, rows, each, True, grads_beside)
     grad_k, grad_v, grad_gain = leaving(
-        functools.partial(last_grads_kernel, heads, members), heads,
+        functools.partial(last_grads_kernel, members), (every, every),
         [key_vectors, value_vectors, inner_k, inner_v, later],
         [flat16, flat16], [shape((heads, HEAD_DIM), F32)],
     )

time: 85.8 us -> 79.4 us (0.925)
  the two profiles are of different devices: /device:TPU:0 before, /device:TPU:1 now
where the time goes in v3:
time: 79.4 us; the launch traced here: 79.1 us
  blocking collectives  49 us (62%)
  Pallas kernels  15.8 us (20%)
  starting transfers between devices  9.12 us (11%)
  waiting for transfers between devices  4.4 us (6%)
    all_to_all x2, blocking collectives, exclusive_sums(): return (exchange(running), work)  25.4 us
    all_to_all x2, blocking collectives, exclusive_sums(): got = exchange(shares)  23.6 us
    pallas_call x6, Pallas kernels, leaving(): pl.pallas_call(whole, out_shape=list(outs) + list(near_outs), in_specs=[W...  12 us
    ppermute x1, starting transfers between devices, sums_over_heads(): lax.ppermute(sums, 'head', [(i, (i + step) % count) for i in range(count)])  4.81 us
    ppermute x2, starting transfers between devices, exclusive_sums(): lax.ppermute(total, 'seq', [(i, (i + hop) % count) for i in range(count)])  4.32 us
    ppermute x2, waiting for transfers between devices, exclusive_sums(): lax.ppermute(total, 'seq', [(i, (i + hop) % count) for i in range(count)])  3.41 us
    pallas_call x6, Pallas kernels, call(): pl.pallas_call(kernel, out_shape=out_shape, in_specs=[WHOLE] * len(args),...  1.97 us
    pallas_call x1, Pallas kernels, local_states(): pl.pallas_call(whole, out_shape=[shape((width, HEAD_DIM), BF16)] + outs,...  1.82 us
  transfers between devices with their start and end apart: 3, of which 2 were waited for; matrix products, arithmetic and copies ran while one was open for 0% of the time, Pallas kernels for 6%

profile of v3, /device:TPU:1, one launch (start us, length us, event | category | flops | bytes accessed | tf_op | source)
XLA Modules:
  0.0 79.1 jit_solution(3479634299561766595)
XLA Ops:
  0.6 1.8 %shard_map.92 = (bf16[3072,128]{1,0:T(8,128)(2,1)S(1)}, bf16[128,3072]{1,0:T(8,128)(2,1)S(1)}, f32[128,3072]{1,0:T(8,128)S(1)}) custom-call(bf16[128,3072]{1,0:T(8,128)(2,1)} %refs_0_.6, bf16[128,3072]{1,0:T(8,128)(2,1)} %refs_1_.15, bf16[128,3072]{1,0:T(8,128)(2,1)} %refs_0_.5), custom_call_target="tpu_custom_call" | custom-call | tf_op jit(solution)/shard_map/pallas_call | solution.py:147
  2.5 0.0 copy-start
  2.5 0.0 copy-start.1
  2.5 11.7 %all_to_all.20.got_ref.refs_0_ = bf16[8,384,128]{2,1,0:T(8,128)(2,1)S(1)} all-to-all(bf16[8,384,128]{2,1,0:T(8,128)(2,1)S(1)} %bitcast.7), channel_id=1, replica_groups={{6,4,12,8,2,0,14,10},{22,20,28,24,18,16,30,26},{7,5,13,9,3,1,15,11},{23..., dimensions={0} | all-to-all | bytes 1572864 | tf_op jit(solution)/shard_map/all_to_all | solution.py:316
  14.2 0.1 shard_map.93
  14.3 2.4 %collective-permute-start = (bf16[384,128]{1,0:T(8,128)(2,1)S(1)}, bf16[384,128]{1,0:T(8,128)(2,1)S(1)}, u32[]{:S(2)}, u32[]{:S(2)}) collective-permute-start(bf16[384,128]{1,0:T(8,128)(2,1)S(1)} %shard_map.93), channel_id=1, source_target_pairs={{0,16},{2,18},{4,20},{6,22},{8,24},{10,26},{12,28},{14,30},{16,0},... | collective-permute-start | bytes 294920 | tf_op jit(solution)/shard_map/ppermute | solution.py:324
  16.7 4.6 %shard_map.94 = (bf16[128,3072]{1,0:T(8,128)(2,1)S(1)}, f32[128,3072]{1,0:T(8,128)S(1)}) custom-call(bf16[128,3072]{1,0:T(8,128)(2,1)S(1)} %copy-done, bf16[128,3072]{1,0:T(8,128)(2,1)S(1)} %copy-done.2, bf16[128,3072]{1,0:T(8,128)(2,1)S(1)} %copy-done.1, ...), custom_call_target="tpu_custom_call", output_to_operand_aliasing={{0}: (3, {}), {1}: (4, {})} | custom-call | tf_op jit(solution)/shard_map/pallas_call | solution.py:92
  21.3 0.1 shard_map.95
  21.4 11.7 %all_to_all.21 = bf16[8,384,128]{2,1,0:T(8,128)(2,1)S(1)} all-to-all(bf16[8,384,128]{2,1,0:T(8,128)(2,1)S(1)} %shard_map.95), channel_id=1, replica_groups={{6,4,12,8,2,0,14,10},{22,20,28,24,18,16,30,26},{7,5,13,9,3,1,15,11},{23..., dimensions={0} | all-to-all | bytes 1572864 | tf_op jit(solution)/shard_map/all_to_all | solution.py:332
  33.1 0.5 shard_map.96
  33.7 4.8 %collective-permute-start.1 = (f32[2,128,128]{2,1,0:T(8,128)S(1)}, f32[2,128,128]{2,1,0:T(8,128)S(1)}, u32[]{:S(2)}, u32[]{:S(2)}) collective-permute-start(f32[2,128,128]{2,1,0:T(8,128)S(1)} %get-tuple-element.42.refs_4_.refs_6_), channel_id=1, source_target_pairs={{0,1},{1,0},{2,3},{3,2},{4,5},{5,4},{6,7},{7,6},{8,9},{9,8},{10,11... | collective-permute-start | bytes 393224 | tf_op jit(solution)/shard_map/ppermute | solution.py:338
  38.5 1.0 %collective-permute-done.1.refs_5_.refs_7_ = f32[2,128,128]{2,1,0:T(8,128)S(1)} collective-permute-done((f32[2,128,128]{2,1,0:T(8,128)S(1)}, f32[2,128,128]{2,1,0:T(8,128)S(1)}, u32[]{:S(2)}, u32[]{:S(2)}) %collective-permute-start.1) | collective-permute-done | bytes 131104 | tf_op jit(solution)/shard_map/ppermute | solution.py:338
  39.5 0.9 %shard_map.97 = (bf16[128,3072]{1,0:T(8,128)(2,1)S(1)}, bf16[8,400,128]{2,1,0:T(8,128)(2,1)S(1)}) custom-call(f32[128,3072]{1,0:T(8,128)S(1)} %get-tuple-element.41.refs_0_.refs_4_, bf16[128,3072]{1,0:T(8,128)(2,1)S(1)} %copy-done.3, f32[24,128]{1,0:T(8,128)S(1)} %bitcast.9, bf16[128,3072]{1,0:T(8,128)(2,1)S(1)} %copy-done, ...), custom_call_target="tpu_custom_call" | custom-call | tf_op jit(solution)/shard_map/pallas_call | solution.py:23
  40.4 2.8 %shard_map.98 = (bf16[128,3072]{1,0:T(8,128)(2,1)S(1)}, f32[128,3072]{1,0:T(8,128)S(1)}, f32[128,3072]{1,0:T(8,128)S(1)}) custom-call(bf16[128,3072]{1,0:T(8,128)(2,1)S(1)} %copy-done, bf16[128,3072]{1,0:T(8,128)(2,1)S(1)} %copy-done.1, bf16[128,3072]{1,0:T(8,128)(2,1)S(1)} %get-tuple-element.58.refs_2_, bf16[128,3072]{1,0:T(8,128)(2,1)S(1)} %get-tuple-element.46.refs_3_), custom_call_target="tpu_custom_call" | custom-call | tf_op jit(solution)/shard_map/pallas_call | solution.py:92
  43.2 2.3 %shard_map.99 = (bf16[128,3072]{1,0:T(8,128)(2,1)}, bf16[128,3072]{1,0:T(8,128)(2,1)}) custom-call(bf16[128,3072]{1,0:T(8,128)(2,1)S(1)} %get-tuple-element.47.refs_0_.refs_4_, bf16[128,3072]{1,0:T(8,128)(2,1)S(1)} %copy-done.2, bf16[128,3072]{1,0:T(8,128)(2,1)S(1)} %get-tuple-element.58.refs_2_, bf16[3072,128]{1,0:T(8,128)(2,1)S(1)} %bitcast.5, ...), custom_call_target="tpu_custom_call" | custom-call | tf_op jit(solution)/shard_map/pallas_call | solution.py:92
  45.5 11.9 %all_to_all.22.got_ref.refs_0_ = bf16[8,400,128]{2,1,0:T(8,128)(2,1)S(1)} all-to-all(bf16[8,400,128]{2,1,0:T(8,128)(2,1)S(1)} %get-tuple-element.53), channel_id=1, replica_groups={{6,4,12,8,2,0,14,10},{22,20,28,24,18,16,30,26},{7,5,13,9,3,1,15,11},{23..., dimensions={0} | all-to-all | bytes 1638400 | tf_op jit(solution)/shard_map/all_to_all | solution.py:316
  57.4 0.1 shard_map.100
  57.5 1.9 %collective-permute-start.2 = (bf16[400,128]{1,0:T(8,128)(2,1)S(1)}, bf16[400,128]{1,0:T(8,128)(2,1)S(1)}, u32[]{:S(2)}, u32[]{:S(2)}) collective-permute-start(bf16[400,128]{1,0:T(8,128)(2,1)S(1)} %shard_map.100), channel_id=1, source_target_pairs={{0,16},{2,18},{4,20},{6,22},{8,24},{10,26},{12,28},{14,30},{16,0},... | collective-permute-start | bytes 307208 | tf_op jit(solution)/shard_map/ppermute | solution.py:324
  59.4 0.1 shard_map.101
  59.6 0.1 shard_map.102
  59.7 3.4 %collective-permute-done.2.refs_1_ = bf16[400,128]{1,0:T(8,128)(2,1)S(1)} collective-permute-done((bf16[400,128]{1,0:T(8,128)(2,1)S(1)}, bf16[400,128]{1,0:T(8,128)(2,1)S(1)}, u32[]{:S(2)}, u32[]{:S(2)}) %collective-permute-start.2) | collective-permute-done | bytes 102432 | tf_op jit(solution)/shard_map/ppermute | solution.py:324
  63.1 0.2 shard_map.103
  63.2 13.7 %all_to_all.23.refs_4_ = bf16[8,400,128]{2,1,0:T(8,128)(2,1)S(1)} all-to-all(bf16[8,400,128]{2,1,0:T(8,128)(2,1)S(1)} %shard_map.103), channel_id=1, replica_groups={{6,4,12,8,2,0,14,10},{22,20,28,24,18,16,30,26},{7,5,13,9,3,1,15,11},{23..., dimensions={0} | all-to-all | bytes 1638400 | tf_op jit(solution)/shard_map/all_to_all | solution.py:332
  76.9 2.2 %shard_map.104 = (bf16[128,3072]{1,0:T(8,128)(2,1)}, bf16[128,3072]{1,0:T(8,128)(2,1)}, f32[24,128]{1,0:T(8,128)}) custom-call(bf16[128,3072]{1,0:T(8,128)(2,1)S(1)} %copy-done.2, bf16[128,3072]{1,0:T(8,128)(2,1)S(1)} %copy-done.1, f32[128,3072]{1,0:T(8,128)S(1)} %get-tuple-element.56.refs_2_, f32[128,3072]{1,0:T(8,128)S(1)} %get-tuple-element.57.refs_3_, ...), custom_call_target="tpu_custom_call" | custom-call | tf_op jit(solution)/shard_map/pallas_call | solution.py:92
  (9 shorter events, 0.0 us)
Async XLA Ops:
  2.5 14.2 %copy-start = (bf16[128,3072]{1,0:T(8,128)(2,1)S(1)}, bf16[128,3072]{1,0:T(8,128)(2,1)}, u32[]{:S(2)}) copy-start(bf16[128,3072]{1,0:T(8,128)(2,1)} %refs_0_.5) | copy-start | bytes 2359300
  2.5 14.2 %copy-start.1 = (bf16[128,3072]{1,0:T(8,128)(2,1)S(1)}, bf16[128,3072]{1,0:T(8,128)(2,1)}, u32[]{:S(2)}) copy-start(bf16[128,3072]{1,0:T(8,128)(2,1)} %refs_1_.15) | copy-start | bytes 2359300
  2.5 14.2 %copy-start.2 = (bf16[128,3072]{1,0:T(8,128)(2,1)S(1)}, bf16[128,3072]{1,0:T(8,128)(2,1)}, u32[]{:S(2)}) copy-start(bf16[128,3072]{1,0:T(8,128)(2,1)} %refs_0_.6) | copy-start | bytes 2359300
  14.3 7.0 %collective-permute-start = (bf16[384,128]{1,0:T(8,128)(2,1)S(1)}, bf16[384,128]{1,0:T(8,128)(2,1)S(1)}, u32[]{:S(2)}, u32[]{:S(2)}) collective-permute-start(bf16[384,128]{1,0:T(8,128)(2,1)S(1)} %shard_map.93), channel_id=1, source_target_pairs={{0,16},{2,18},{4,20},{6,22},{8,24},{10,26},{12,28},{14,30},{16,0},... | collective-permute-start | bytes 294920 | tf_op jit(solution)/shard_map/ppermute | solution.py:324
  21.2 11.9 %copy-start.3 = (bf16[128,3072]{1,0:T(8,128)(2,1)S(1)}, bf16[128,3072]{1,0:T(8,128)(2,1)}, u32[]{:S(2)}) copy-start(bf16[128,3072]{1,0:T(8,128)(2,1)} %refs_1_.10) | copy-start | bytes 2359300
  21.3 11.9 %copy-start.4 = (f32[3072]{0:T(1024)S(1)}, f32[3072]{0:T(1024)}, u32[]{:S(2)}) copy-start(f32[3072]{0:T(1024)} %param.8) | copy-start | bytes 36868
  33.7 5.8 %collective-permute-start.1 = (f32[2,128,128]{2,1,0:T(8,128)S(1)}, f32[2,128,128]{2,1,0:T(8,128)S(1)}, u32[]{:S(2)}, u32[]{:S(2)}) collective-permute-start(f32[2,128,128]{2,1,0:T(8,128)S(1)} %get-tuple-element.42.refs_4_.refs_6_), channel_id=1, source_target_pairs={{0,1},{1,0},{2,3},{3,2},{4,5},{5,4},{6,7},{7,6},{8,9},{9,8},{10,11... | collective-permute-start | bytes 393224 | tf_op jit(solution)/shard_map/ppermute | solution.py:338
  57.5 5.6 %collective-permute-start.2 = (bf16[400,128]{1,0:T(8,128)(2,1)S(1)}, bf16[400,128]{1,0:T(8,128)(2,1)S(1)}, u32[]{:S(2)}, u32[]{:S(2)}) collective-permute-start(bf16[400,128]{1,0:T(8,128)(2,1)S(1)} %shard_map.100), channel_id=1, source_target_pairs={{0,16},{2,18},{4,20},{6,22},{8,24},{10,26},{12,28},{14,30},{16,0},... | collective-permute-start | bytes 307208 | tf_op jit(solution)/shard_map/ppermute | solution.py:324

commit v4 on v3

--- a/solution.py
+++ b/solution.py
@@ -29,6 +29,20 @@
     )(*args)
 
 
+def first_core(mine, other):
+    odd = lax.axis_index("head") % 2
+    pl.when(odd == 0)(mine)
+    pl.when(odd == 1)(other)
+
+
+def call_on(first, kernel, out_shape, *args):
+    def whole(*refs):
+        work, rest = lambda: kernel(*refs), lambda: None
+        first_core(work if first else rest, rest if first else work)
+
+    return call(whole, out_shape, *args)
+
+
 def dot(a, b, over):
     return lax.dot_general(a, b, ((over[:1], over[1:]), ((), ())), preferred_element_type=F32)
 
@@ -46,12 +60,6 @@
     rows = lax.broadcasted_iota(jnp.int32, (length, length), 0)
     cols = lax.broadcasted_iota(jnp.int32, (length, length), 1)
     return cols <= rows
-
-
-def first_core(mine, other):
-    odd = lax.axis_index("head") % 2
-    pl.when(odd == 0)(mine)
-    pl.when(odd == 1)(other)
 
 
 def leave(kernel, span, ins, outs, buffers, sems, blocks):
@@ -75,7 +83,7 @@
         copy.wait()
 
 
-def leaving(kernel, spans, ins, outs, near_outs=(), held=(), blocks=4):
+def leaving(kernels, spans, ins, outs, near_outs=(), held=(), blocks=4):
     count = len(outs)
 
     def whole(*refs):
@@ -83,11 +91,11 @@
         out_refs, refs = refs[:count], refs[count:]
         near_refs, refs = refs[:len(near_outs)], refs[len(near_outs):]
         buffers, sems = refs[:count], refs[count]
-        work = lambda span: leave(kernel, span, in_refs + near_refs, out_refs, buffers, sems, blocks)
-        if spans[0] == spans[1]:
-            work(spans[0])
-        else:
-            first_core(lambda: work(spans[0]), lambda: work(spans[1]))
+        work = [
+            functools.partial(leave, kernel, span, in_refs + near_refs, out_refs, buffers, sems, blocks)
+            for kernel, span in zip(kernels, spans)
+        ]
+        first_core(*work)
 
     return pl.pallas_call(
         whole,
@@ -100,18 +108,16 @@
     )(*ins, *held)
 
 
-def inner_out_kernel(span, done, query_ref, key_ref, value_ref, weights_ref, inner_ref):
+def inner_out_kernel(heads, query_ref, key_ref, value_ref, weights_ref, inner_ref):
     mask = causal_mask(query_ref.shape[0])
-    for h in span:
-        cols = columns(h)
-        scores = dot(query_ref[:, cols], key_ref[:, cols], (1, 1))
-        weights = jnp.where(mask, scores, 0.0).astype(BF16)
-        weights_ref[:, cols] = weights
-        inner_ref[:, cols] = dot(weights, value_ref[:, cols], (1, 0))
-        done(h)
-
-
-def local_states(heads, early, queries, key_vectors, value_vectors, outs, blocks=2):
+    for h in range(heads):
+        scores = dot(query_ref[:, columns(h)], key_ref[:, columns(h)], (1, 1))
+        weights_ref[:, columns(h)] = jnp.where(mask, scores, 0.0).astype(BF16)
+    for h in range(heads):
+        inner_ref[:, columns(h)] = dot(weights_ref[:, columns(h)], value_ref[:, columns(h)], (1, 0))
+
+
+def local_states(heads, queries, key_vectors, value_vectors, outs, blocks=2):
     length, width = key_vectors.shape
     while heads % blocks:
         blocks -= 1
@@ -120,51 +126,53 @@
 
     def whole(*refs):
         far, (state_ref, *out_refs) = refs[:3], refs[3:6]
-        key_ref, value_ref, query_ref, weights_ref, inner_ref, in_sems, out_sems = refs[6:]
+        key_ref, value_ref, query_ref, sems, query_sem = refs[6:]
         arrivals = []
         for block in range(blocks):
             cols = pl.ds(block * step * HEAD_DIM, step * HEAD_DIM)
             for i, (ref, buffer) in enumerate(((far[0], key_ref), (far[1], value_ref))):
-                arrivals.append(pltpu.make_async_copy(ref.at[:, cols], buffer.at[:, cols], in_sems.at[i, block]))
-        cols = pl.ds(0, max(len(early), 1) * HEAD_DIM)
-        query_copy = pltpu.make_async_copy(far[2].at[:, cols], query_ref.at[:, cols], in_sems.at[2, 0])
+                arrivals.append(pltpu.make_async_copy(ref.at[:, cols], buffer.at[:, cols], sems.at[i, block]))
+        query_copy = pltpu.make_async_copy(far[2], query_ref, query_sem)
         for copy in arrivals:
             copy.start()
-        query_copy.start()
+        first_core(query_copy.start, lambda: None)
         for h in range(heads):
             if h % step == 0:
                 for copy in arrivals[2 * (h // step):2 * (h // step) + 2]:
                     copy.wait()
             part = dot(key_ref[:, columns(h)], value_ref[:, columns(h)], (0, 0))
             state_ref[columns(h), :] = part.astype(BF16)
-        query_copy.wait()
-        ins = query_ref, key_ref, value_ref
-        first_core(
-            lambda: leave(inner_out_kernel, early, ins, out_refs, (weights_ref, inner_ref), out_sems, 1),
-            lambda: None,
-        )
+
+        def early():
+            query_copy.wait()
+            inner_out_kernel(heads, query_ref, key_ref, value_ref, *out_refs)
+
+        first_core(early, lambda: None)
 
     return pl.pallas_call(
         whole,
         out_shape=[shape((width, HEAD_DIM), BF16)] + outs,
         in_specs=[FAR] * 3,
-        out_specs=[WHOLE, FAR, FAR],
-        scratch_shapes=[pltpu.VMEM((length, width), BF16)] * 3 + [pltpu.VMEM(a.shape, a.dtype) for a in outs]
-        + [pltpu.SemaphoreType.DMA((3, blocks)), pltpu.SemaphoreType.DMA((1, 2))],
+        out_specs=[WHOLE] * 3,
+        scratch_shapes=[pltpu.VMEM((length, width), BF16)] * 3
+        + [pltpu.SemaphoreType.DMA((2, blocks)), pltpu.SemaphoreType.DMA],
         compiler_params=pltpu.CompilerParams(vmem_limit_bytes=VMEM_LIMIT),
     )(*sources)
 
 
-def out_kernel(heads, query_ref, inner_ref, up_ref, prior_ref, gain_ref, out_ref, sums_ref):
-    squares = jnp.zeros(sums_ref.shape[1:], F32)
-    products = jnp.zeros(sums_ref.shape[1:], F32)
-    for h in range(heads):
-        out = inner_ref[:, columns(h)] + dot(query_ref[:, columns(h)], prior_ref[columns(h), :], (1, 0))
-        out_ref[:, columns(h)] = out
-        squares += out * out
-        products += up_ref[:, columns(h)].astype(F32) * gain_ref[h][None] * out
-    sums_ref[0] = squares
-    sums_ref[1] = products
+def out_kernel(heads, query_ref, first_inner_ref, second_inner_ref, up_ref, prior_ref, gain_ref, out_ref, sums_ref):
+    def work(inner_ref):
+        squares = jnp.zeros(sums_ref.shape[1:], F32)
+        products = jnp.zeros(sums_ref.shape[1:], F32)
+        for h in range(heads):
+            out = inner_ref[:, columns(h)] + dot(query_ref[:, columns(h)], prior_ref[columns(h), :], (1, 0))
+            out_ref[:, columns(h)] = out
+            squares += out * out
+            products += up_ref[:, columns(h)].astype(F32) * gain_ref[h][None] * out
+        sums_ref[0] = squares
+        sums_ref[1] = products
+
+    first_core(lambda: work(first_inner_ref), lambda: work(second_inner_ref))
 
 
 def token_factors(total_width, sums_refs):
@@ -207,17 +215,16 @@
             gains = []
 
 
-def inner_grads_kernel(span, done, *refs):
-    query_ref, value_ref, grad_ref, weights_ref, scores_ref, inner_k_ref, inner_v_ref = refs
+def inner_grads_kernel(span, done, query_ref, value_ref, grad_ref, weights_ref, scores_ref, inner_k_ref, inner_v_ref):
     mask = causal_mask(query_ref.shape[0])
     for h in span:
         cols = columns(h)
-        grad = grad_ref[:, cols]
-        scores = dot(grad, value_ref[:, cols], (1, 1))
-        scores = jnp.where(mask, scores, 0.0).astype(BF16)
-        scores_ref[:, cols] = scores
-        inner_k_ref[:, cols] = dot(scores, query_ref[:, cols], (0, 0))
-        inner_v_ref[:, cols] = dot(weights_ref[:, cols], grad, (0, 0))
+        scores = dot(grad_ref[:, cols], value_ref[:, cols], (1, 1))
+        scores_ref[:, cols] = jnp.where(mask, scores, 0.0).astype(BF16)
+    for h in span:
+        cols = columns(h)
+        inner_k_ref[:, cols] = dot(scores_ref[:, cols], query_ref[:, cols], (0, 0))
+        inner_v_ref[:, cols] = dot(weights_ref[:, cols], grad_ref[:, cols], (0, 0))
         done(h)
 
 
@@ -233,8 +240,9 @@
         done(h)
 
 
-def last_grads_kernel(parts, span, done, *refs):
-    key_ref, value_ref, inner_k_ref, inner_v_ref, got_ref, gain_ref, grad_k_ref, grad_v_ref = refs
+def last_grads_kernel(parts, first, span, done, *refs):
+    key_ref, value_ref, got_ref, *inner_refs, gain_ref, grad_k_ref, grad_v_ref = refs
+    inner_k_ref, inner_v_ref = inner_refs[:2] if first else inner_refs[2:]
     heads = len(span)
     rows = heads * HEAD_DIM // parts
     each = gain_rows(heads, parts)
@@ -362,22 +370,24 @@
     flat32 = shape((length, width), F32)
     flat_scores = shape((length, heads * length), BF16)
 
-    every, none, early = range(heads), range(0), range(heads // 2)
-    state, *held = local_states(heads, early, queries, key_vectors, value_vectors, [flat_scores, flat32])
-
-    def inner_out(got, total):
-        weights, inner = leaving(
-            inner_out_kernel, (every[len(early):], every),
-            [tied(queries, total), key_vectors, value_vectors], [flat_scores, flat32], (), held,
+    every, none = range(heads), range(0)
+    inner_out = functools.partial(inner_out_kernel, heads)
+    state, weights, inner = local_states(heads, queries, key_vectors, value_vectors, [flat_scores, flat32])
+
+    def inner_out_beside(got, total):
+        results = call_on(
+            False, inner_out, [flat_scores, flat32], tied(queries, total), key_vectors, value_vectors
         )
-        return tied(got, inner), (weights, inner)
-
-    prior, (weights, inner) = exclusive_sums(state.reshape(members, rows, HEAD_DIM), rows, 0, False, inner_out)
+        return tied(got, results), results
+
+    prior, (second_weights, second_inner) = exclusive_sums(
+        state.reshape(members, rows, HEAD_DIM), rows, 0, False, inner_out_beside
+    )
     prior = prior.reshape(width, HEAD_DIM)
     out, sums = call(
         functools.partial(out_kernel, heads),
         [flat32, shape((2, length, HEAD_DIM), F32)],
-        queries, inner, upstream, prior, gain,
+        queries, inner, second_inner, upstream, prior, gain,
     )
     sums = sums_over_heads(sums)
     each = gain_rows(heads, members)
@@ -388,31 +398,33 @@
         out, upstream, gain, queries, *sums,
     )
 
-    def inner_grads(spans, after, held=(), blocks=4):
-        return leaving(
-            inner_grads_kernel, spans, [tied(queries, after), value_vectors, grad, weights],
-            [flat_scores, flat32, flat32], (), held, blocks,
-        )
+    inner_shapes = [flat_scores, flat32, flat32]
 
     def query_grads(spans, after, scores, held=(), blocks=4):
         return leaving(
-            functools.partial(query_grads_kernel, total_width), spans,
+            [functools.partial(query_grads_kernel, total_width)] * 2, spans,
             [scores, key_vectors, tied(grad, after), prior, out, gain, *sums], [flat16, flat16], (), held, blocks,
         )
 
-    first = inner_grads((none, every), shares)
-    ready = query_grads((none, every), first, first[0], (), 1)
-    shares = tied(shares, ready)
+    second_scores, *second_inner = leaving(
+        [inner_grads_kernel] * 2, (none, every),
+        [tied(queries, shares), value_vectors, grad, second_weights], inner_shapes, (), (), 8,
+    )
+    held = query_grads((none, every), second_inner, second_scores, (), 1)
+    shares = tied(shares, held)
 
     def grads_beside(got, total):
-        late = inner_grads((every, none), total, first)
-        results = query_grads((every, none), late, late[0], ready)
-        return tied(got, results), (late, results)
-
-    later, ((_, inner_k, inner_v), (attended, grad_q)) = exclusive_sums(shares, rows, each, True, grads_beside)
+        scores, *inner = call_on(
+            True, functools.partial(inner_grads_kernel, every, lambda h: None), inner_shapes,
+            tied(queries, total), value_vectors, grad, weights,
+        )
+        results = query_grads((every, none), inner, scores, held)
+        return tied(got, results), (inner, results)
+
+    later, (inner, (attended, grad_q)) = exclusive_sums(shares, rows, each, True, grads_beside)
     grad_k, grad_v, grad_gain = leaving(
-        functools.partial(last_grads_kernel, members), (every, every),
-        [key_vectors, value_vectors, inner_k, inner_v, later],
+        [functools.partial(last_grads_kernel, members, first) for first in (True, False)], (every, every),
+        [key_vectors, value_vectors, later, *inner, *second_inner],
         [flat16, flat16], [shape((heads, HEAD_DIM), F32)],
     )
     return attended, grad_q, grad_k, grad_v, grad_gain.reshape(-1)

time: 79.4 us -> 78.8 us (level)
  Pallas kernels: 15.8 us -> 12.7 us
  starting transfers between devices: 9.12 us -> 11.1 us
    pallas_call x6 -> x4, Pallas kernels: 12 us -> 8.01 us  [leaving(): pl.pallas_call(whole, out_shape=list(outs) + list(near_outs), in_specs=[W...]
    ppermute x2, starting transfers between devices: 4.32 us -> 5.71 us  [exclusive_sums(): lax.ppermute(total, 'seq', [(i, (i + hop) % count) for i in range(count)])]
    pallas_call x6 -> x8, Pallas kernels: 1.97 us -> 2.94 us  [call(): pl.pallas_call(kernel, out_shape=out_shape, in_specs=[WHOLE] * len(args),...]
  transfers between devices with their start and end apart: 3 -> 3, of which waited for: 2 -> 3; matrix products, arithmetic and copies ran while one was open for 0% -> 0% of each run, Pallas kernels for 6% -> 1%
where the time goes in v4:
time: 78.8 us; the launch traced here: 78.5 us
  blocking collectives  49.5 us (63%)
  Pallas kernels  12.7 us (16%)
  starting transfers between devices  11.1 us (14%)
  waiting for transfers between devices  4.33 us (5%)
    all_to_all x2, blocking collectives, exclusive_sums(): return (exchange(running), work)  25.3 us
    all_to_all x2, blocking collectives, exclusive_sums(): got = exchange(shares)  24.3 us
    pallas_call x4, Pallas kernels, leaving(): pl.pallas_call(whole, out_shape=list(outs) + list(near_outs), in_specs=[W...  8.01 us
    ppermute x2, starting transfers between devices, exclusive_sums(): lax.ppermute(total, 'seq', [(i, (i + hop) % count) for i in range(count)])  5.71 us
    ppermute x1, starting transfers between devices, sums_over_heads(): lax.ppermute(sums, 'head', [(i, (i + step) % count) for i in range(count)])  5.44 us
    ppermute x2, waiting for transfers between devices, exclusive_sums(): lax.ppermute(total, 'seq', [(i, (i + hop) % count) for i in range(count)])  3.35 us
    pallas_call x8, Pallas kernels, call(): pl.pallas_call(kernel, out_shape=out_shape, in_specs=[WHOLE] * len(args),...  2.94 us
    pallas_call x1, Pallas kernels, local_states(): pl.pallas_call(whole, out_shape=[shape((width, HEAD_DIM), BF16)] + outs,...  1.78 us
  transfers between devices with their start and end apart: 3, of which 3 were waited for; matrix products, arithmetic and copies ran while one was open for 0% of the time, Pallas kernels for 1%

profile of v4, /device:TPU:1, one launch (start us, length us, event | category | flops | bytes accessed | tf_op | source)
XLA Modules:
  0.0 78.5 jit_solution(14366480079408574834)
XLA Ops:
  0.6 1.8 %shard_map.92 = (bf16[3072,128]{1,0:T(8,128)(2,1)S(1)}, bf16[128,3072]{1,0:T(8,128)(2,1)S(1)}, f32[128,3072]{1,0:T(8,128)S(1)}) custom-call(bf16[128,3072]{1,0:T(8,128)(2,1)} %refs_0_.6, bf16[128,3072]{1,0:T(8,128)(2,1)} %refs_1_.15, bf16[128,3072]{1,0:T(8,128)(2,1)} %refs_0_.5), custom_call_target="tpu_custom_call" | custom-call | tf_op jit(solution)/shard_map/pallas_call | solution.py:152
  2.4 0.0 copy-start
  2.4 0.0 copy-start.1
  2.5 12.8 %all_to_all.20.got_ref.refs_0_ = bf16[8,384,128]{2,1,0:T(8,128)(2,1)S(1)} all-to-all(bf16[8,384,128]{2,1,0:T(8,128)(2,1)S(1)} %bitcast.7), channel_id=1, replica_groups={{6,4,12,8,2,0,14,10},{22,20,28,24,18,16,30,26},{7,5,13,9,3,1,15,11},{23..., dimensions={0} | all-to-all | bytes 1572864 | tf_op jit(solution)/shard_map/all_to_all | solution.py:324
  15.3 0.1 shard_map.93
  15.4 2.4 %collective-permute-start = (bf16[384,128]{1,0:T(8,128)(2,1)S(1)}, bf16[384,128]{1,0:T(8,128)(2,1)S(1)}, u32[]{:S(2)}, u32[]{:S(2)}) collective-permute-start(bf16[384,128]{1,0:T(8,128)(2,1)S(1)} %shard_map.93), channel_id=1, source_target_pairs={{0,16},{2,18},{4,20},{6,22},{8,24},{10,26},{12,28},{14,30},{16,0},... | collective-permute-start | bytes 294920 | tf_op jit(solution)/shard_map/ppermute | solution.py:332
  17.8 0.9 %shard_map.94 = (bf16[128,3072]{1,0:T(8,128)(2,1)S(1)}, f32[128,3072]{1,0:T(8,128)S(1)}) custom-call(bf16[128,3072]{1,0:T(8,128)(2,1)S(1)} %copy-done, bf16[128,3072]{1,0:T(8,128)(2,1)S(1)} %copy-done.2, bf16[128,3072]{1,0:T(8,128)(2,1)S(1)} %copy-done.1), custom_call_target="tpu_custom_call" | custom-call | tf_op jit(solution)/shard_map/pallas_call | solution.py:23
  18.7 1.1 %collective-permute-done.refs_1_ = bf16[384,128]{1,0:T(8,128)(2,1)S(1)} collective-permute-done((bf16[384,128]{1,0:T(8,128)(2,1)S(1)}, bf16[384,128]{1,0:T(8,128)(2,1)S(1)}, u32[]{:S(2)}, u32[]{:S(2)}) %collective-permute-start) | collective-permute-done | bytes 98336 | tf_op jit(solution)/shard_map/ppermute | solution.py:332
  19.8 0.1 shard_map.95
  20.0 12.1 %all_to_all.21 = bf16[8,384,128]{2,1,0:T(8,128)(2,1)S(1)} all-to-all(bf16[8,384,128]{2,1,0:T(8,128)(2,1)S(1)} %shard_map.95), channel_id=1, replica_groups={{6,4,12,8,2,0,14,10},{22,20,28,24,18,16,30,26},{7,5,13,9,3,1,15,11},{23..., dimensions={0} | all-to-all | bytes 1572864 | tf_op jit(solution)/shard_map/all_to_all | solution.py:340
  32.1 0.6 shard_map.96
  32.7 5.4 %collective-permute-start.1 = (f32[2,128,128]{2,1,0:T(8,128)S(1)}, f32[2,128,128]{2,1,0:T(8,128)S(1)}, u32[]{:S(2)}, u32[]{:S(2)}) collective-permute-start(f32[2,128,128]{2,1,0:T(8,128)S(1)} %get-tuple-element.42.refs_4_.refs_6_), channel_id=1, source_target_pairs={{0,1},{1,0},{2,3},{3,2},{4,5},{5,4},{6,7},{7,6},{8,9},{9,8},{10,11... | collective-permute-start | bytes 393224 | tf_op jit(solution)/shard_map/ppermute | solution.py:346
  38.1 1.0 %collective-permute-done.1.refs_5_.refs_7_ = f32[2,128,128]{2,1,0:T(8,128)S(1)} collective-permute-done((f32[2,128,128]{2,1,0:T(8,128)S(1)}, f32[2,128,128]{2,1,0:T(8,128)S(1)}, u32[]{:S(2)}, u32[]{:S(2)}) %collective-permute-start.1) | collective-permute-done | bytes 131104 | tf_op jit(solution)/shard_map/ppermute | solution.py:346
  39.1 0.9 %shard_map.97 = (bf16[128,3072]{1,0:T(8,128)(2,1)S(1)}, bf16[8,400,128]{2,1,0:T(8,128)(2,1)S(1)}) custom-call(f32[128,3072]{1,0:T(8,128)S(1)} %get-tuple-element.41.refs_0_.refs_4_, bf16[128,3072]{1,0:T(8,128)(2,1)S(1)} %copy-done.3, f32[24,128]{1,0:T(8,128)S(1)} %bitcast.9, bf16[128,3072]{1,0:T(8,128)(2,1)S(1)} %copy-done, ...), custom_call_target="tpu_custom_call" | custom-call | tf_op jit(solution)/shard_map/pallas_call | solution.py:23
  40.1 3.4 %shard_map.98 = (bf16[128,3072]{1,0:T(8,128)(2,1)S(1)}, f32[128,3072]{1,0:T(8,128)S(1)}, f32[128,3072]{1,0:T(8,128)S(1)}) custom-call(bf16[128,3072]{1,0:T(8,128)(2,1)S(1)} %copy-done, bf16[128,3072]{1,0:T(8,128)(2,1)S(1)} %copy-done.1, bf16[128,3072]{1,0:T(8,128)(2,1)S(1)} %get-tuple-element.58.refs_2_, bf16[128,3072]{1,0:T(8,128)(2,1)S(1)} %get-tuple-element.39.refs_3_), custom_call_target="tpu_custom_call" | custom-call | tf_op jit(solution)/shard_map/pallas_call | solution.py:100
  43.5 2.3 %shard_map.99 = (bf16[128,3072]{1,0:T(8,128)(2,1)}, bf16[128,3072]{1,0:T(8,128)(2,1)}) custom-call(bf16[128,3072]{1,0:T(8,128)(2,1)S(1)} %get-tuple-element.46.refs_0_, bf16[128,3072]{1,0:T(8,128)(2,1)S(1)} %copy-done.2, bf16[128,3072]{1,0:T(8,128)(2,1)S(1)} %get-tuple-element.58.refs_2_, bf16[3072,128]{1,0:T(8,128)(2,1)S(1)} %bitcast.5, ...), custom_call_target="tpu_custom_call" | custom-call | tf_op jit(solution)/shard_map/pallas_call | solution.py:100
  45.8 11.4 %all_to_all.22.got_ref.refs_0_ = bf16[8,400,128]{2,1,0:T(8,128)(2,1)S(1)} all-to-all(bf16[8,400,128]{2,1,0:T(8,128)(2,1)S(1)} %get-tuple-element.52), channel_id=1, replica_groups={{6,4,12,8,2,0,14,10},{22,20,28,24,18,16,30,26},{7,5,13,9,3,1,15,11},{23..., dimensions={0} | all-to-all | bytes 1638400 | tf_op jit(solution)/shard_map/all_to_all | solution.py:324
  57.2 0.1 shard_map.100
  57.4 3.3 %collective-permute-start.2 = (bf16[400,128]{1,0:T(8,128)(2,1)S(1)}, bf16[400,128]{1,0:T(8,128)(2,1)S(1)}, u32[]{:S(2)}, u32[]{:S(2)}) collective-permute-start(bf16[400,128]{1,0:T(8,128)(2,1)S(1)} %shard_map.100), channel_id=1, source_target_pairs={{0,16},{2,18},{4,20},{6,22},{8,24},{10,26},{12,28},{14,30},{16,0},... | collective-permute-start | bytes 307208 | tf_op jit(solution)/shard_map/ppermute | solution.py:332
  60.7 0.1 shard_map.102
  60.8 2.2 %collective-permute-done.2.refs_1_ = bf16[400,128]{1,0:T(8,128)(2,1)S(1)} collective-permute-done((bf16[400,128]{1,0:T(8,128)(2,1)S(1)}, bf16[400,128]{1,0:T(8,128)(2,1)S(1)}, u32[]{:S(2)}, u32[]{:S(2)}) %collective-permute-start.2) | collective-permute-done | bytes 102432 | tf_op jit(solution)/shard_map/ppermute | solution.py:332
  63.0 0.2 shard_map.103
  63.2 13.1 %all_to_all.23.refs_2_ = bf16[8,400,128]{2,1,0:T(8,128)(2,1)S(1)} all-to-all(bf16[8,400,128]{2,1,0:T(8,128)(2,1)S(1)} %shard_map.103), channel_id=1, replica_groups={{6,4,12,8,2,0,14,10},{22,20,28,24,18,16,30,26},{7,5,13,9,3,1,15,11},{23..., dimensions={0} | all-to-all | bytes 1638400 | tf_op jit(solution)/shard_map/all_to_all | solution.py:340
  76.3 2.2 %shard_map.104 = (bf16[128,3072]{1,0:T(8,128)(2,1)}, bf16[128,3072]{1,0:T(8,128)(2,1)}, f32[24,128]{1,0:T(8,128)}) custom-call(bf16[128,3072]{1,0:T(8,128)(2,1)S(1)} %copy-done.2, bf16[128,3072]{1,0:T(8,128)(2,1)S(1)} %copy-done.1, bf16[8,400,128]{2,1,0:T(8,128)(2,1)S(1)} %all_to_all.23.refs_2_, f32[128,3072]{1,0:T(8,128)S(1)} %get-tuple-element.56.refs_3_, ...), custom_call_target="tpu_custom_call" | custom-call | tf_op jit(solution)/shard_map/pallas_call | solution.py:100
  (9 shorter events, 0.0 us)
Async XLA Ops:
  2.4 15.4 %copy-start = (bf16[128,3072]{1,0:T(8,128)(2,1)S(1)}, bf16[128,3072]{1,0:T(8,128)(2,1)}, u32[]{:S(2)}) copy-start(bf16[128,3072]{1,0:T(8,128)(2,1)} %refs_0_.5) | copy-start | bytes 2359300
  2.4 15.4 %copy-start.1 = (bf16[128,3072]{1,0:T(8,128)(2,1)S(1)}, bf16[128,3072]{1,0:T(8,128)(2,1)}, u32[]{:S(2)}) copy-start(bf16[128,3072]{1,0:T(8,128)(2,1)} %refs_1_.15) | copy-start | bytes 2359300
  2.4 15.3 %copy-start.2 = (bf16[128,3072]{1,0:T(8,128)(2,1)S(1)}, bf16[128,3072]{1,0:T(8,128)(2,1)}, u32[]{:S(2)}) copy-start(bf16[128,3072]{1,0:T(8,128)(2,1)} %refs_0_.6) | copy-start | bytes 2359300
  15.4 4.4 %collective-permute-start = (bf16[384,128]{1,0:T(8,128)(2,1)S(1)}, bf16[384,128]{1,0:T(8,128)(2,1)S(1)}, u32[]{:S(2)}, u32[]{:S(2)}) collective-permute-start(bf16[384,128]{1,0:T(8,128)(2,1)S(1)} %shard_map.93), channel_id=1, source_target_pairs={{0,16},{2,18},{4,20},{6,22},{8,24},{10,26},{12,28},{14,30},{16,0},... | collective-permute-start | bytes 294920 | tf_op jit(solution)/shard_map/ppermute | solution.py:332
  18.7 13.4 %copy-start.3 = (bf16[128,3072]{1,0:T(8,128)(2,1)S(1)}, bf16[128,3072]{1,0:T(8,128)(2,1)}, u32[]{:S(2)}) copy-start(bf16[128,3072]{1,0:T(8,128)(2,1)} %refs_1_.10) | copy-start | bytes 2359300
  18.7 13.4 %copy-start.4 = (f32[3072]{0:T(1024)S(1)}, f32[3072]{0:T(1024)}, u32[]{:S(2)}) copy-start(f32[3072]{0:T(1024)} %param.8) | copy-start | bytes 36868
  32.7 6.4 %collective-permute-start.1 = (f32[2,128,128]{2,1,0:T(8,128)S(1)}, f32[2,128,128]{2,1,0:T(8,128)S(1)}, u32[]{:S(2)}, u32[]{:S(2)}) collective-permute-start(f32[2,128,128]{2,1,0:T(8,128)S(1)} %get-tuple-element.42.refs_4_.refs_6_), channel_id=1, source_target_pairs={{0,1},{1,0},{2,3},{3,2},{4,5},{5,4},{6,7},{7,6},{8,9},{9,8},{10,11... | collective-permute-start | bytes 393224 | tf_op jit(solution)/shard_map/ppermute | solution.py:346
  57.4 5.7 %collective-permute-start.2 = (bf16[400,128]{1,0:T(8,128)(2,1)S(1)}, bf16[400,128]{1,0:T(8,128)(2,1)S(1)}, u32[]{:S(2)}, u32[]{:S(2)}) collective-permute-start(bf16[400,128]{1,0:T(8,128)(2,1)S(1)} %shard_map.100), channel_id=1, source_target_pairs={{0,16},{2,18},{4,20},{6,22},{8,24},{10,26},{12,28},{14,30},{16,0},... | collective-permute-start | bytes 307208 | tf_op jit(solution)/shard_map/ppermute | solution.py:332

commit v5 on v4

--- a/solution.py
+++ b/solution.py
@@ -260,9 +260,10 @@
         grad_v = inner_v_ref[:, cols] + dot(key_ref[:, cols], later, (1, 0))
         grad_v_ref[:, cols] = grad_v.astype(BF16)
         done(h)
-        part, row = divmod(h, each)
+    for part in range(-(-heads // each)):
         pair = got_ref[part, rows:rows + 2 * each, :].astype(F32)
-        gain_ref[h:h + 1, :] = pair[row:row + 1] + pair[each + row:each + row + 1]
+        own = min(each, heads - part * each)
+        gain_ref[part * each:part * each + own, :] = pair[:own] + pair[each:each + own]
 
 
 def gain_sum(rows, each, value):
@@ -309,7 +310,7 @@
 
 
 def member_order(members):
-    quick = (3, 2, 6, 4, 1, 0, 7, 5)
+    quick = (3, 1, 5, 6, 7, 4, 0, 2)
     return list(quick if len(quick) == members else range(members))
 
 
@@ -425,7 +426,7 @@
     grad_k, grad_v, grad_gain = leaving(
         [functools.partial(last_grads_kernel, members, first) for first in (True, False)], (every, every),
         [key_vectors, value_vectors, later, *inner, *second_inner],
-        [flat16, flat16], [shape((heads, HEAD_DIM), F32)],
+        [flat16, flat16], [shape((heads, HEAD_DIM), F32)], (), 6
     )
     return attended, grad_q, grad_k, grad_v, grad_gain.reshape(-1)
 

time: 78.8 us -> 78.1 us (level)
  blocking collectives: 49.5 us -> 47.9 us
  waiting for transfers between devices: 4.33 us -> 5.25 us
    all_to_all x2, blocking collectives: 25.3 us -> 23.4 us  [exclusive_sums(): return (exchange(running), work)]
    ppermute x2, waiting for transfers between devices: 3.35 us -> 4.26 us  [exclusive_sums(): lax.ppermute(total, 'seq', [(i, (i + hop) % count) for i in range(count)])]
where the time goes in v5:
time: 78.1 us; the launch traced here: 77.8 us
  blocking collectives  47.9 us (61%)
  Pallas kernels  12.7 us (16%)
  starting transfers between devices  11.2 us (14%)
  waiting for transfers between devices  5.25 us (7%)
    all_to_all x2, blocking collectives, exclusive_sums(): got = exchange(shares)  24.5 us
    all_to_all x2, blocking collectives, exclusive_sums(): return (exchange(running), work)  23.4 us
    pallas_call x4, Pallas kernels, leaving(): pl.pallas_call(whole, out_shape=list(outs) + list(near_outs), in_specs=[W...  8 us
    ppermute x2, starting transfers between devices, exclusive_sums(): lax.ppermute(total, 'seq', [(i, (i + hop) % count) for i in range(count)])  6.11 us
    ppermute x1, starting transfers between devices, sums_over_heads(): lax.ppermute(sums, 'head', [(i, (i + step) % count) for i in range(count)])  5.1 us
    ppermute x2, waiting for transfers between devices, exclusive_sums(): lax.ppermute(total, 'seq', [(i, (i + hop) % count) for i in range(count)])  4.26 us
    pallas_call x8, Pallas kernels, call(): pl.pallas_call(kernel, out_shape=out_shape, in_specs=[WHOLE] * len(args),...  2.94 us
    pallas_call x1, Pallas kernels, local_states(): pl.pallas_call(whole, out_shape=[shape((width, HEAD_DIM), BF16)] + outs,...  1.78 us
  transfers between devices with their start and end apart: 3, of which 3 were waited for; matrix products, arithmetic and copies ran while one was open for 0% of the time, Pallas kernels for 1%

profile of v5, /device:TPU:1, one launch (start us, length us, event | category | flops | bytes accessed | tf_op | source)
XLA Modules:
  0.0 77.8 jit_solution(16167042617234822415)
XLA Ops:
  0.6 1.8 %shard_map.92 = (bf16[3072,128]{1,0:T(8,128)(2,1)S(1)}, bf16[128,3072]{1,0:T(8,128)(2,1)S(1)}, f32[128,3072]{1,0:T(8,128)S(1)}) custom-call(bf16[128,3072]{1,0:T(8,128)(2,1)} %refs_0_.6, bf16[128,3072]{1,0:T(8,128)(2,1)} %refs_1_.15, bf16[128,3072]{1,0:T(8,128)(2,1)} %refs_0_.5), custom_call_target="tpu_custom_call" | custom-call | tf_op jit(solution)/shard_map/pallas_call | solution.py:152
  2.4 0.0 copy-start
  2.4 0.0 copy-start.1
  2.5 14.2 %all_to_all.20.got_ref.refs_0_ = bf16[8,384,128]{2,1,0:T(8,128)(2,1)S(1)} all-to-all(bf16[8,384,128]{2,1,0:T(8,128)(2,1)S(1)} %bitcast.7), channel_id=1, replica_groups={{6,2,10,12,14,8,0,4},{22,18,26,28,30,24,16,20},{7,3,11,13,15,9,1,5},{23..., dimensions={0} | all-to-all | bytes 1572864 | tf_op jit(solution)/shard_map/all_to_all | solution.py:325
  16.7 0.1 shard_map.93
  16.8 2.4 %collective-permute-start = (bf16[384,128]{1,0:T(8,128)(2,1)S(1)}, bf16[384,128]{1,0:T(8,128)(2,1)S(1)}, u32[]{:S(2)}, u32[]{:S(2)}) collective-permute-start(bf16[384,128]{1,0:T(8,128)(2,1)S(1)} %shard_map.93), channel_id=1, source_target_pairs={{0,16},{2,18},{4,20},{6,22},{8,24},{10,26},{12,28},{14,30},{16,0},... | collective-permute-start | bytes 294920 | tf_op jit(solution)/shard_map/ppermute | solution.py:333
  19.2 0.9 %shard_map.94 = (bf16[128,3072]{1,0:T(8,128)(2,1)S(1)}, f32[128,3072]{1,0:T(8,128)S(1)}) custom-call(bf16[128,3072]{1,0:T(8,128)(2,1)S(1)} %copy-done, bf16[128,3072]{1,0:T(8,128)(2,1)S(1)} %copy-done.2, bf16[128,3072]{1,0:T(8,128)(2,1)S(1)} %copy-done.1), custom_call_target="tpu_custom_call" | custom-call | tf_op jit(solution)/shard_map/pallas_call | solution.py:23
  20.1 2.2 %collective-permute-done.refs_1_ = bf16[384,128]{1,0:T(8,128)(2,1)S(1)} collective-permute-done((bf16[384,128]{1,0:T(8,128)(2,1)S(1)}, bf16[384,128]{1,0:T(8,128)(2,1)S(1)}, u32[]{:S(2)}, u32[]{:S(2)}) %collective-permute-start) | collective-permute-done | bytes 98336 | tf_op jit(solution)/shard_map/ppermute | solution.py:333
  22.3 0.1 shard_map.95
  22.4 10.3 %all_to_all.21 = bf16[8,384,128]{2,1,0:T(8,128)(2,1)S(1)} all-to-all(bf16[8,384,128]{2,1,0:T(8,128)(2,1)S(1)} %shard_map.95), channel_id=1, replica_groups={{6,2,10,12,14,8,0,4},{22,18,26,28,30,24,16,20},{7,3,11,13,15,9,1,5},{23..., dimensions={0} | all-to-all | bytes 1572864 | tf_op jit(solution)/shard_map/all_to_all | solution.py:341
  32.7 0.6 shard_map.96
  33.3 5.1 %collective-permute-start.1 = (f32[2,128,128]{2,1,0:T(8,128)S(1)}, f32[2,128,128]{2,1,0:T(8,128)S(1)}, u32[]{:S(2)}, u32[]{:S(2)}) collective-permute-start(f32[2,128,128]{2,1,0:T(8,128)S(1)} %get-tuple-element.42.refs_4_.refs_6_), channel_id=1, source_target_pairs={{0,1},{1,0},{2,3},{3,2},{4,5},{5,4},{6,7},{7,6},{8,9},{9,8},{10,11... | collective-permute-start | bytes 393224 | tf_op jit(solution)/shard_map/ppermute | solution.py:347
  38.4 1.0 %collective-permute-done.1.refs_5_.refs_7_ = f32[2,128,128]{2,1,0:T(8,128)S(1)} collective-permute-done((f32[2,128,128]{2,1,0:T(8,128)S(1)}, f32[2,128,128]{2,1,0:T(8,128)S(1)}, u32[]{:S(2)}, u32[]{:S(2)}) %collective-permute-start.1) | collective-permute-done | bytes 131104 | tf_op jit(solution)/shard_map/ppermute | solution.py:347
  39.4 0.9 %shard_map.97 = (bf16[128,3072]{1,0:T(8,128)(2,1)S(1)}, bf16[8,400,128]{2,1,0:T(8,128)(2,1)S(1)}) custom-call(f32[128,3072]{1,0:T(8,128)S(1)} %get-tuple-element.41.refs_0_.refs_4_, bf16[128,3072]{1,0:T(8,128)(2,1)S(1)} %copy-done.3, f32[24,128]{1,0:T(8,128)S(1)} %bitcast.9, bf16[128,3072]{1,0:T(8,128)(2,1)S(1)} %copy-done, ...), custom_call_target="tpu_custom_call" | custom-call | tf_op jit(solution)/shard_map/pallas_call | solution.py:23
  40.3 3.4 %shard_map.98 = (bf16[128,3072]{1,0:T(8,128)(2,1)S(1)}, f32[128,3072]{1,0:T(8,128)S(1)}, f32[128,3072]{1,0:T(8,128)S(1)}) custom-call(bf16[128,3072]{1,0:T(8,128)(2,1)S(1)} %copy-done, bf16[128,3072]{1,0:T(8,128)(2,1)S(1)} %copy-done.1, bf16[128,3072]{1,0:T(8,128)(2,1)S(1)} %get-tuple-element.58.refs_2_, bf16[128,3072]{1,0:T(8,128)(2,1)S(1)} %get-tuple-element.39.refs_3_), custom_call_target="tpu_custom_call" | custom-call | tf_op jit(solution)/shard_map/pallas_call | solution.py:100
  43.8 2.3 %shard_map.99 = (bf16[128,3072]{1,0:T(8,128)(2,1)}, bf16[128,3072]{1,0:T(8,128)(2,1)}) custom-call(bf16[128,3072]{1,0:T(8,128)(2,1)S(1)} %get-tuple-element.46.refs_0_, bf16[128,3072]{1,0:T(8,128)(2,1)S(1)} %copy-done.2, bf16[128,3072]{1,0:T(8,128)(2,1)S(1)} %get-tuple-element.58.refs_2_, bf16[3072,128]{1,0:T(8,128)(2,1)S(1)} %bitcast.5, ...), custom_call_target="tpu_custom_call" | custom-call | tf_op jit(solution)/shard_map/pallas_call | solution.py:100
  46.1 10.3 %all_to_all.22.got_ref.refs_0_ = bf16[8,400,128]{2,1,0:T(8,128)(2,1)S(1)} all-to-all(bf16[8,400,128]{2,1,0:T(8,128)(2,1)S(1)} %get-tuple-element.52), channel_id=1, replica_groups={{6,2,10,12,14,8,0,4},{22,18,26,28,30,24,16,20},{7,3,11,13,15,9,1,5},{23..., dimensions={0} | all-to-all | bytes 1638400 | tf_op jit(solution)/shard_map/all_to_all | solution.py:325
  56.3 0.1 shard_map.100
  56.5 3.7 %collective-permute-start.2 = (bf16[400,128]{1,0:T(8,128)(2,1)S(1)}, bf16[400,128]{1,0:T(8,128)(2,1)S(1)}, u32[]{:S(2)}, u32[]{:S(2)}) collective-permute-start(bf16[400,128]{1,0:T(8,128)(2,1)S(1)} %shard_map.100), channel_id=1, source_target_pairs={{0,16},{2,18},{4,20},{6,22},{8,24},{10,26},{12,28},{14,30},{16,0},... | collective-permute-start | bytes 307208 | tf_op jit(solution)/shard_map/ppermute | solution.py:333
  60.2 0.1 shard_map.102
  60.3 2.1 %collective-permute-done.2.refs_1_ = bf16[400,128]{1,0:T(8,128)(2,1)S(1)} collective-permute-done((bf16[400,128]{1,0:T(8,128)(2,1)S(1)}, bf16[400,128]{1,0:T(8,128)(2,1)S(1)}, u32[]{:S(2)}, u32[]{:S(2)}) %collective-permute-start.2) | collective-permute-done | bytes 102432 | tf_op jit(solution)/shard_map/ppermute | solution.py:333
  62.4 0.2 shard_map.103
  62.5 13.1 %all_to_all.23.refs_2_ = bf16[8,400,128]{2,1,0:T(8,128)(2,1)S(1)} all-to-all(bf16[8,400,128]{2,1,0:T(8,128)(2,1)S(1)} %shard_map.103), channel_id=1, replica_groups={{6,2,10,12,14,8,0,4},{22,18,26,28,30,24,16,20},{7,3,11,13,15,9,1,5},{23..., dimensions={0} | all-to-all | bytes 1638400 | tf_op jit(solution)/shard_map/all_to_all | solution.py:341
  75.6 2.2 %shard_map.104 = (bf16[128,3072]{1,0:T(8,128)(2,1)}, bf16[128,3072]{1,0:T(8,128)(2,1)}, f32[24,128]{1,0:T(8,128)}) custom-call(bf16[128,3072]{1,0:T(8,128)(2,1)S(1)} %copy-done.2, bf16[128,3072]{1,0:T(8,128)(2,1)S(1)} %copy-done.1, bf16[8,400,128]{2,1,0:T(8,128)(2,1)S(1)} %all_to_all.23.refs_2_, f32[128,3072]{1,0:T(8,128)S(1)} %get-tuple-element.56.refs_3_, ...), custom_call_target="tpu_custom_call" | custom-call | tf_op jit(solution)/shard_map/pallas_call | solution.py:100
  (9 shorter events, 0.0 us)
Async XLA Ops:
  2.4 16.8 %copy-start = (bf16[128,3072]{1,0:T(8,128)(2,1)S(1)}, bf16[128,3072]{1,0:T(8,128)(2,1)}, u32[]{:S(2)}) copy-start(bf16[128,3072]{1,0:T(8,128)(2,1)} %refs_0_.5) | copy-start | bytes 2359300
  2.4 16.7 %copy-start.1 = (bf16[128,3072]{1,0:T(8,128)(2,1)S(1)}, bf16[128,3072]{1,0:T(8,128)(2,1)}, u32[]{:S(2)}) copy-start(bf16[128,3072]{1,0:T(8,128)(2,1)} %refs_1_.15) | copy-start | bytes 2359300
  2.4 16.7 %copy-start.2 = (bf16[128,3072]{1,0:T(8,128)(2,1)S(1)}, bf16[128,3072]{1,0:T(8,128)(2,1)}, u32[]{:S(2)}) copy-start(bf16[128,3072]{1,0:T(8,128)(2,1)} %refs_0_.6) | copy-start | bytes 2359300
  16.8 5.5 %collective-permute-start = (bf16[384,128]{1,0:T(8,128)(2,1)S(1)}, bf16[384,128]{1,0:T(8,128)(2,1)S(1)}, u32[]{:S(2)}, u32[]{:S(2)}) collective-permute-start(bf16[384,128]{1,0:T(8,128)(2,1)S(1)} %shard_map.93), channel_id=1, source_target_pairs={{0,16},{2,18},{4,20},{6,22},{8,24},{10,26},{12,28},{14,30},{16,0},... | collective-permute-start | bytes 294920 | tf_op jit(solution)/shard_map/ppermute | solution.py:333
  20.1 12.6 %copy-start.3 = (bf16[128,3072]{1,0:T(8,128)(2,1)S(1)}, bf16[128,3072]{1,0:T(8,128)(2,1)}, u32[]{:S(2)}) copy-start(bf16[128,3072]{1,0:T(8,128)(2,1)} %refs_1_.10) | copy-start | bytes 2359300
  20.1 12.6 %copy-start.4 = (f32[3072]{0:T(1024)S(1)}, f32[3072]{0:T(1024)}, u32[]{:S(2)}) copy-start(f32[3072]{0:T(1024)} %param.8) | copy-start | bytes 36868
  33.3 6.1 %collective-permute-start.1 = (f32[2,128,128]{2,1,0:T(8,128)S(1)}, f32[2,128,128]{2,1,0:T(8,128)S(1)}, u32[]{:S(2)}, u32[]{:S(2)}) collective-permute-start(f32[2,128,128]{2,1,0:T(8,128)S(1)} %get-tuple-element.42.refs_4_.refs_6_), channel_id=1, source_target_pairs={{0,1},{1,0},{2,3},{3,2},{4,5},{5,4},{6,7},{7,6},{8,9},{9,8},{10,11... | collective-permute-start | bytes 393224 | tf_op jit(solution)/shard_map/ppermute | solution.py:347
  56.5 5.9 %collective-permute-start.2 = (bf16[400,128]{1,0:T(8,128)(2,1)S(1)}, bf16[400,128]{1,0:T(8,128)(2,1)S(1)}, u32[]{:S(2)}, u32[]{:S(2)}) collective-permute-start(bf16[400,128]{1,0:T(8,128)(2,1)S(1)} %shard_map.100), channel_id=1, source_target_pairs={{0,16},{2,18},{4,20},{6,22},{8,24},{10,26},{12,28},{14,30},{16,0},... | collective-permute-start | bytes 307208 | tf_op jit(solution)/shard_map/ppermute | solution.py:333

commit v6 on v5

--- a/solution.py
+++ b/solution.py
@@ -299,7 +299,7 @@
         gain = gain_sum(rows, each, jnp.sum(got_ref[...].astype(F32), axis=0))
         for ref in total_refs:
             gain += gain_sum(rows, each, ref[...].astype(F32))
-    order = member_order(members)
+    order = member_order(members, reverse)
     for block in range(members - 1, -1, -1) if reverse else range(members):
         member = order.index(block)
         if each:
@@ -309,8 +309,8 @@
         state += got_ref[member, :rows, :].astype(F32)
 
 
-def member_order(members):
-    quick = (3, 1, 5, 6, 7, 4, 0, 2)
+def member_order(members, reverse):
+    quick = (3, 2, 6, 4, 1, 0, 7, 5) if reverse else (3, 1, 6, 5, 7, 4, 0, 2)
     return list(quick if len(quick) == members else range(members))
 
 
@@ -318,7 +318,7 @@
     count = lax.axis_size("seq")
     members = shares.shape[0]
     groups = count // members
-    index_groups = [[g * members + block for block in member_order(members)] for g in range(groups)]
+    index_groups = [[g * members + block for block in member_order(members, reverse)] for g in range(groups)]
     exchange = functools.partial(
         lax.all_to_all, axis_name="seq", split_axis=0, concat_axis=0, axis_index_groups=index_groups, tiled=True
     )

time: 78.1 us -> 78 us (level)
  no operation moved by 1% of the time
where the time goes in v6:
time: 78 us; the launch traced here: 77.7 us
  blocking collectives  47.8 us (61%)
  Pallas kernels  12.7 us (16%)
  starting transfers between devices  11.2 us (14%)
  waiting for transfers between devices  5.29 us (7%)
    all_to_all x2, blocking collectives, exclusive_sums(): got = exchange(shares)  24.5 us
    all_to_all x2, blocking collectives, exclusive_sums(): return (exchange(running), work)  23.2 us
    pallas_call x4, Pallas kernels, leaving(): pl.pallas_call(whole, out_shape=list(outs) + list(near_outs), in_specs=[W...  8 us
    ppermute x2, starting transfers between devices, exclusive_sums(): lax.ppermute(total, 'seq', [(i, (i + hop) % count) for i in range(count)])  6.13 us
    ppermute x1, starting transfers between devices, sums_over_heads(): lax.ppermute(sums, 'head', [(i, (i + step) % count) for i in range(count)])  5.06 us
    ppermute x2, waiting for transfers between devices, exclusive_sums(): lax.ppermute(total, 'seq', [(i, (i + hop) % count) for i in range(count)])  4.3 us
    pallas_call x8, Pallas kernels, call(): pl.pallas_call(kernel, out_shape=out_shape, in_specs=[WHOLE] * len(args),...  2.94 us
    pallas_call x1, Pallas kernels, local_states(): pl.pallas_call(whole, out_shape=[shape((width, HEAD_DIM), BF16)] + outs,...  1.78 us
  transfers between devices with their start and end apart: 3, of which 3 were waited for; matrix products, arithmetic and copies ran while one was open for 0% of the time, Pallas kernels for 1%

profile of v6, /device:TPU:1, one launch (start us, length us, event | category | flops | bytes accessed | tf_op | source)
XLA Modules:
  0.0 77.7 jit_solution(7452536379204940005)
XLA Ops:
  0.6 1.8 %shard_map.92 = (bf16[3072,128]{1,0:T(8,128)(2,1)S(1)}, bf16[128,3072]{1,0:T(8,128)(2,1)S(1)}, f32[128,3072]{1,0:T(8,128)S(1)}) custom-call(bf16[128,3072]{1,0:T(8,128)(2,1)} %refs_0_.6, bf16[128,3072]{1,0:T(8,128)(2,1)} %refs_1_.15, bf16[128,3072]{1,0:T(8,128)(2,1)} %refs_0_.5), custom_call_target="tpu_custom_call" | custom-call | tf_op jit(solution)/shard_map/pallas_call | solution.py:152
  2.4 0.0 copy-start
  2.4 0.0 copy-start.1
  2.5 14.2 %all_to_all.20.got_ref.refs_0_ = bf16[8,384,128]{2,1,0:T(8,128)(2,1)S(1)} all-to-all(bf16[8,384,128]{2,1,0:T(8,128)(2,1)S(1)} %bitcast.7), channel_id=1, replica_groups={{6,2,12,10,14,8,0,4},{22,18,28,26,30,24,16,20},{7,3,13,11,15,9,1,5},{23..., dimensions={0} | all-to-all | bytes 1572864 | tf_op jit(solution)/shard_map/all_to_all | solution.py:325
  16.7 0.1 shard_map.93
  16.8 2.4 %collective-permute-start = (bf16[384,128]{1,0:T(8,128)(2,1)S(1)}, bf16[384,128]{1,0:T(8,128)(2,1)S(1)}, u32[]{:S(2)}, u32[]{:S(2)}) collective-permute-start(bf16[384,128]{1,0:T(8,128)(2,1)S(1)} %shard_map.93), channel_id=1, source_target_pairs={{0,16},{2,18},{4,20},{6,22},{8,24},{10,26},{12,28},{14,30},{16,0},... | collective-permute-start | bytes 294920 | tf_op jit(solution)/shard_map/ppermute | solution.py:333
  19.2 0.9 %shard_map.94 = (bf16[128,3072]{1,0:T(8,128)(2,1)S(1)}, f32[128,3072]{1,0:T(8,128)S(1)}) custom-call(bf16[128,3072]{1,0:T(8,128)(2,1)S(1)} %copy-done, bf16[128,3072]{1,0:T(8,128)(2,1)S(1)} %copy-done.2, bf16[128,3072]{1,0:T(8,128)(2,1)S(1)} %copy-done.1), custom_call_target="tpu_custom_call" | custom-call | tf_op jit(solution)/shard_map/pallas_call | solution.py:23
  20.1 2.2 %collective-permute-done.refs_1_ = bf16[384,128]{1,0:T(8,128)(2,1)S(1)} collective-permute-done((bf16[384,128]{1,0:T(8,128)(2,1)S(1)}, bf16[384,128]{1,0:T(8,128)(2,1)S(1)}, u32[]{:S(2)}, u32[]{:S(2)}) %collective-permute-start) | collective-permute-done | bytes 98336 | tf_op jit(solution)/shard_map/ppermute | solution.py:333
  22.3 0.1 shard_map.95
  22.4 10.3 %all_to_all.21 = bf16[8,384,128]{2,1,0:T(8,128)(2,1)S(1)} all-to-all(bf16[8,384,128]{2,1,0:T(8,128)(2,1)S(1)} %shard_map.95), channel_id=1, replica_groups={{6,2,12,10,14,8,0,4},{22,18,28,26,30,24,16,20},{7,3,13,11,15,9,1,5},{23..., dimensions={0} | all-to-all | bytes 1572864 | tf_op jit(solution)/shard_map/all_to_all | solution.py:341
  32.8 0.6 shard_map.96
  33.4 5.1 %collective-permute-start.1 = (f32[2,128,128]{2,1,0:T(8,128)S(1)}, f32[2,128,128]{2,1,0:T(8,128)S(1)}, u32[]{:S(2)}, u32[]{:S(2)}) collective-permute-start(f32[2,128,128]{2,1,0:T(8,128)S(1)} %get-tuple-element.42.refs_4_.refs_6_), channel_id=1, source_target_pairs={{0,1},{1,0},{2,3},{3,2},{4,5},{5,4},{6,7},{7,6},{8,9},{9,8},{10,11... | collective-permute-start | bytes 393224 | tf_op jit(solution)/shard_map/ppermute | solution.py:347
  38.4 1.0 %collective-permute-done.1.refs_5_.refs_7_ = f32[2,128,128]{2,1,0:T(8,128)S(1)} collective-permute-done((f32[2,128,128]{2,1,0:T(8,128)S(1)}, f32[2,128,128]{2,1,0:T(8,128)S(1)}, u32[]{:S(2)}, u32[]{:S(2)}) %collective-permute-start.1) | collective-permute-done | bytes 131104 | tf_op jit(solution)/shard_map/ppermute | solution.py:347
  39.4 0.9 %shard_map.97 = (bf16[128,3072]{1,0:T(8,128)(2,1)S(1)}, bf16[8,400,128]{2,1,0:T(8,128)(2,1)S(1)}) custom-call(f32[128,3072]{1,0:T(8,128)S(1)} %get-tuple-element.41.refs_0_.refs_4_, bf16[128,3072]{1,0:T(8,128)(2,1)S(1)} %copy-done.3, f32[24,128]{1,0:T(8,128)S(1)} %bitcast.9, bf16[128,3072]{1,0:T(8,128)(2,1)S(1)} %copy-done, ...), custom_call_target="tpu_custom_call" | custom-call | tf_op jit(solution)/shard_map/pallas_call | solution.py:23
  40.3 3.4 %shard_map.98 = (bf16[128,3072]{1,0:T(8,128)(2,1)S(1)}, f32[128,3072]{1,0:T(8,128)S(1)}, f32[128,3072]{1,0:T(8,128)S(1)}) custom-call(bf16[128,3072]{1,0:T(8,128)(2,1)S(1)} %copy-done, bf16[128,3072]{1,0:T(8,128)(2,1)S(1)} %copy-done.1, bf16[128,3072]{1,0:T(8,128)(2,1)S(1)} %get-tuple-element.58.refs_2_, bf16[128,3072]{1,0:T(8,128)(2,1)S(1)} %get-tuple-element.39.refs_3_), custom_call_target="tpu_custom_call" | custom-call | tf_op jit(solution)/shard_map/pallas_call | solution.py:100
  43.8 2.3 %shard_map.99 = (bf16[128,3072]{1,0:T(8,128)(2,1)}, bf16[128,3072]{1,0:T(8,128)(2,1)}) custom-call(bf16[128,3072]{1,0:T(8,128)(2,1)S(1)} %get-tuple-element.46.refs_0_, bf16[128,3072]{1,0:T(8,128)(2,1)S(1)} %copy-done.2, bf16[128,3072]{1,0:T(8,128)(2,1)S(1)} %get-tuple-element.58.refs_2_, bf16[3072,128]{1,0:T(8,128)(2,1)S(1)} %bitcast.5, ...), custom_call_target="tpu_custom_call" | custom-call | tf_op jit(solution)/shard_map/pallas_call | solution.py:100
  46.1 10.3 %all_to_all.22.got_ref.refs_0_ = bf16[8,400,128]{2,1,0:T(8,128)(2,1)S(1)} all-to-all(bf16[8,400,128]{2,1,0:T(8,128)(2,1)S(1)} %get-tuple-element.52), channel_id=1, replica_groups={{6,4,12,8,2,0,14,10},{22,20,28,24,18,16,30,26},{7,5,13,9,3,1,15,11},{23..., dimensions={0} | all-to-all | bytes 1638400 | tf_op jit(solution)/shard_map/all_to_all | solution.py:325
  56.3 0.1 shard_map.100
  56.4 3.8 %collective-permute-start.2 = (bf16[400,128]{1,0:T(8,128)(2,1)S(1)}, bf16[400,128]{1,0:T(8,128)(2,1)S(1)}, u32[]{:S(2)}, u32[]{:S(2)}) collective-permute-start(bf16[400,128]{1,0:T(8,128)(2,1)S(1)} %shard_map.100), channel_id=1, source_target_pairs={{0,16},{2,18},{4,20},{6,22},{8,24},{10,26},{12,28},{14,30},{16,0},... | collective-permute-start | bytes 307208 | tf_op jit(solution)/shard_map/ppermute | solution.py:333
  60.2 0.1 shard_map.102
  60.3 2.1 %collective-permute-done.2.refs_1_ = bf16[400,128]{1,0:T(8,128)(2,1)S(1)} collective-permute-done((bf16[400,128]{1,0:T(8,128)(2,1)S(1)}, bf16[400,128]{1,0:T(8,128)(2,1)S(1)}, u32[]{:S(2)}, u32[]{:S(2)}) %collective-permute-start.2) | collective-permute-done | bytes 102432 | tf_op jit(solution)/shard_map/ppermute | solution.py:333
  62.4 0.2 shard_map.103
  62.6 12.9 %all_to_all.23.refs_2_ = bf16[8,400,128]{2,1,0:T(8,128)(2,1)S(1)} all-to-all(bf16[8,400,128]{2,1,0:T(8,128)(2,1)S(1)} %shard_map.103), channel_id=1, replica_groups={{6,4,12,8,2,0,14,10},{22,20,28,24,18,16,30,26},{7,5,13,9,3,1,15,11},{23..., dimensions={0} | all-to-all | bytes 1638400 | tf_op jit(solution)/shard_map/all_to_all | solution.py:341
  75.5 2.2 %shard_map.104 = (bf16[128,3072]{1,0:T(8,128)(2,1)}, bf16[128,3072]{1,0:T(8,128)(2,1)}, f32[24,128]{1,0:T(8,128)}) custom-call(bf16[128,3072]{1,0:T(8,128)(2,1)S(1)} %copy-done.2, bf16[128,3072]{1,0:T(8,128)(2,1)S(1)} %copy-done.1, bf16[8,400,128]{2,1,0:T(8,128)(2,1)S(1)} %all_to_all.23.refs_2_, f32[128,3072]{1,0:T(8,128)S(1)} %get-tuple-element.56.refs_3_, ...), custom_call_target="tpu_custom_call" | custom-call | tf_op jit(solution)/shard_map/pallas_call | solution.py:100
  (9 shorter events, 0.0 us)
Async XLA Ops:
  2.4 16.8 %copy-start = (bf16[128,3072]{1,0:T(8,128)(2,1)S(1)}, bf16[128,3072]{1,0:T(8,128)(2,1)}, u32[]{:S(2)}) copy-start(bf16[128,3072]{1,0:T(8,128)(2,1)} %refs_0_.5) | copy-start | bytes 2359300
  2.4 16.7 %copy-start.1 = (bf16[128,3072]{1,0:T(8,128)(2,1)S(1)}, bf16[128,3072]{1,0:T(8,128)(2,1)}, u32[]{:S(2)}) copy-start(bf16[128,3072]{1,0:T(8,128)(2,1)} %refs_1_.15) | copy-start | bytes 2359300
  2.4 16.7 %copy-start.2 = (bf16[128,3072]{1,0:T(8,128)(2,1)S(1)}, bf16[128,3072]{1,0:T(8,128)(2,1)}, u32[]{:S(2)}) copy-start(bf16[128,3072]{1,0:T(8,128)(2,1)} %refs_0_.6) | copy-start | bytes 2359300
  16.8 5.5 %collective-permute-start = (bf16[384,128]{1,0:T(8,128)(2,1)S(1)}, bf16[384,128]{1,0:T(8,128)(2,1)S(1)}, u32[]{:S(2)}, u32[]{:S(2)}) collective-permute-start(bf16[384,128]{1,0:T(8,128)(2,1)S(1)} %shard_map.93), channel_id=1, source_target_pairs={{0,16},{2,18},{4,20},{6,22},{8,24},{10,26},{12,28},{14,30},{16,0},... | collective-permute-start | bytes 294920 | tf_op jit(solution)/shard_map/ppermute | solution.py:333
  20.1 12.7 %copy-start.3 = (bf16[128,3072]{1,0:T(8,128)(2,1)S(1)}, bf16[128,3072]{1,0:T(8,128)(2,1)}, u32[]{:S(2)}) copy-start(bf16[128,3072]{1,0:T(8,128)(2,1)} %refs_1_.10) | copy-start | bytes 2359300
  20.1 12.7 %copy-start.4 = (f32[3072]{0:T(1024)S(1)}, f32[3072]{0:T(1024)}, u32[]{:S(2)}) copy-start(f32[3072]{0:T(1024)} %param.8) | copy-start | bytes 36868
  33.4 6.0 %collective-permute-start.1 = (f32[2,128,128]{2,1,0:T(8,128)S(1)}, f32[2,128,128]{2,1,0:T(8,128)S(1)}, u32[]{:S(2)}, u32[]{:S(2)}) collective-permute-start(f32[2,128,128]{2,1,0:T(8,128)S(1)} %get-tuple-element.42.refs_4_.refs_6_), channel_id=1, source_target_pairs={{0,1},{1,0},{2,3},{3,2},{4,5},{5,4},{6,7},{7,6},{8,9},{9,8},{10,11... | collective-permute-start | bytes 393224 | tf_op jit(solution)/shard_map/ppermute | solution.py:347
  56.4 6.0 %collective-permute-start.2 = (bf16[400,128]{1,0:T(8,128)(2,1)S(1)}, bf16[400,128]{1,0:T(8,128)(2,1)S(1)}, u32[]{:S(2)}, u32[]{:S(2)}) collective-permute-start(bf16[400,128]{1,0:T(8,128)(2,1)S(1)} %shard_map.100), channel_id=1, source_target_pairs={{0,16},{2,18},{4,20},{6,22},{8,24},{10,26},{12,28},{14,30},{16,0},... | collective-permute-start | bytes 307208 | tf_op jit(solution)/shard_map/ppermute | solution.py:333

commit v7 on v5

--- a/solution.py
+++ b/solution.py
@@ -162,23 +162,24 @@
 
 def out_kernel(heads, query_ref, first_inner_ref, second_inner_ref, up_ref, prior_ref, gain_ref, out_ref, sums_ref):
     def work(inner_ref):
-        squares = jnp.zeros(sums_ref.shape[1:], F32)
-        products = jnp.zeros(sums_ref.shape[1:], F32)
+        squares = jnp.zeros(sums_ref.shape, F32)
+        products = jnp.zeros(sums_ref.shape, F32)
         for h in range(heads):
             out = inner_ref[:, columns(h)] + dot(query_ref[:, columns(h)], prior_ref[columns(h), :], (1, 0))
             out_ref[:, columns(h)] = out
             squares += out * out
             products += up_ref[:, columns(h)].astype(F32) * gain_ref[h][None] * out
-        sums_ref[0] = squares
-        sums_ref[1] = products
+        half = HEAD_DIM // 2
+        fold = lambda value: value[:, :half] + value[:, half:]
+        sums_ref[...] = jnp.concatenate([fold(squares), fold(products)], axis=1)
 
     first_core(lambda: work(first_inner_ref), lambda: work(second_inner_ref))
 
 
 def token_factors(total_width, sums_refs):
     sums = functools.reduce(lambda a, b: a + b, [ref[...] for ref in sums_refs])
-    inv = lax.rsqrt(jnp.sum(sums[0], axis=1, keepdims=True) / total_width + 1e-6)
-    mean_dot = jnp.sum(sums[1], axis=1, keepdims=True) / total_width * inv
+    inv = lax.rsqrt(jnp.sum(sums[:, :HEAD_DIM // 2], axis=1, keepdims=True) / total_width + 1e-6)
+    mean_dot = jnp.sum(sums[:, HEAD_DIM // 2:], axis=1, keepdims=True) / total_width * inv
     return inv, mean_dot
 
 
@@ -387,7 +388,7 @@
     prior = prior.reshape(width, HEAD_DIM)
     out, sums = call(
         functools.partial(out_kernel, heads),
-        [flat32, shape((2, length, HEAD_DIM), F32)],
+        [flat32, shape((length, HEAD_DIM), F32)],
         queries, inner, second_inner, upstream, prior, gain,
     )
     sums = sums_over_heads(sums)

time: 78.1 us -> 78.2 us (level)
  no operation moved by 1% of the time
where the time goes in v7:
time: 78.2 us; the launch traced here: 77.9 us
  blocking collectives  47.9 us (61%)
  Pallas kernels  12.8 us (16%)
  starting transfers between devices  11.2 us (14%)
  waiting for transfers between devices  5.16 us (7%)
    all_to_all x2, blocking collectives, exclusive_sums(): got = exchange(shares)  24.5 us
    all_to_all x2, blocking collectives, exclusive_sums(): return (exchange(running), work)  23.4 us
    pallas_call x4, Pallas kernels, leaving(): pl.pallas_call(whole, out_shape=list(outs) + list(near_outs), in_specs=[W...  7.96 us
    ppermute x2, starting transfers between devices, exclusive_sums(): lax.ppermute(total, 'seq', [(i, (i + hop) % count) for i in range(count)])  6.11 us
    ppermute x1, starting transfers between devices, sums_over_heads(): lax.ppermute(sums, 'head', [(i, (i + step) % count) for i in range(count)])  5.13 us
    ppermute x2, waiting for transfers between devices, exclusive_sums(): lax.ppermute(total, 'seq', [(i, (i + hop) % count) for i in range(count)])  4.26 us
    pallas_call x8, Pallas kernels, call(): pl.pallas_call(kernel, out_shape=out_shape, in_specs=[WHOLE] * len(args),...  3.09 us
    pallas_call x1, Pallas kernels, local_states(): pl.pallas_call(whole, out_shape=[shape((width, HEAD_DIM), BF16)] + outs,...  1.78 us
  transfers between devices with their start and end apart: 3, of which 3 were waited for; matrix products, arithmetic and copies ran while one was open for 0% of the time, Pallas kernels for 1%

profile of v7, /device:TPU:1, one launch (start us, length us, event | category | flops | bytes accessed | tf_op | source)
XLA Modules:
  0.0 77.9 jit_solution(13146819877446290143)
XLA Ops:
  0.6 1.8 %shard_map.92 = (bf16[3072,128]{1,0:T(8,128)(2,1)S(1)}, bf16[128,3072]{1,0:T(8,128)(2,1)S(1)}, f32[128,3072]{1,0:T(8,128)S(1)}) custom-call(bf16[128,3072]{1,0:T(8,128)(2,1)} %refs_0_.6, bf16[128,3072]{1,0:T(8,128)(2,1)} %refs_1_.15, bf16[128,3072]{1,0:T(8,128)(2,1)} %refs_0_.5), custom_call_target="tpu_custom_call" | custom-call | tf_op jit(solution)/shard_map/pallas_call | solution.py:152
  2.4 0.0 copy-start
  2.4 0.0 copy-start.1
  2.5 14.2 %all_to_all.20.got_ref.refs_0_ = bf16[8,384,128]{2,1,0:T(8,128)(2,1)S(1)} all-to-all(bf16[8,384,128]{2,1,0:T(8,128)(2,1)S(1)} %bitcast.7), channel_id=1, replica_groups={{6,2,10,12,14,8,0,4},{22,18,26,28,30,24,16,20},{7,3,11,13,15,9,1,5},{23..., dimensions={0} | all-to-all | bytes 1572864 | tf_op jit(solution)/shard_map/all_to_all | solution.py:326
  16.7 0.1 shard_map.93
  16.8 2.4 %collective-permute-start = (bf16[384,128]{1,0:T(8,128)(2,1)S(1)}, bf16[384,128]{1,0:T(8,128)(2,1)S(1)}, u32[]{:S(2)}, u32[]{:S(2)}) collective-permute-start(bf16[384,128]{1,0:T(8,128)(2,1)S(1)} %shard_map.93), channel_id=1, source_target_pairs={{0,16},{2,18},{4,20},{6,22},{8,24},{10,26},{12,28},{14,30},{16,0},... | collective-permute-start | bytes 294920 | tf_op jit(solution)/shard_map/ppermute | solution.py:334
  19.2 0.9 %shard_map.94 = (bf16[128,3072]{1,0:T(8,128)(2,1)S(1)}, f32[128,3072]{1,0:T(8,128)S(1)}) custom-call(bf16[128,3072]{1,0:T(8,128)(2,1)S(1)} %copy-done, bf16[128,3072]{1,0:T(8,128)(2,1)S(1)} %copy-done.2, bf16[128,3072]{1,0:T(8,128)(2,1)S(1)} %copy-done.1), custom_call_target="tpu_custom_call" | custom-call | tf_op jit(solution)/shard_map/pallas_call | solution.py:23
  20.1 2.2 %collective-permute-done.refs_1_ = bf16[384,128]{1,0:T(8,128)(2,1)S(1)} collective-permute-done((bf16[384,128]{1,0:T(8,128)(2,1)S(1)}, bf16[384,128]{1,0:T(8,128)(2,1)S(1)}, u32[]{:S(2)}, u32[]{:S(2)}) %collective-permute-start) | collective-permute-done | bytes 98336 | tf_op jit(solution)/shard_map/ppermute | solution.py:334
  22.3 0.1 shard_map.95
  22.4 10.3 %all_to_all.21 = bf16[8,384,128]{2,1,0:T(8,128)(2,1)S(1)} all-to-all(bf16[8,384,128]{2,1,0:T(8,128)(2,1)S(1)} %shard_map.95), channel_id=1, replica_groups={{6,2,10,12,14,8,0,4},{22,18,26,28,30,24,16,20},{7,3,11,13,15,9,1,5},{23..., dimensions={0} | all-to-all | bytes 1572864 | tf_op jit(solution)/shard_map/all_to_all | solution.py:342
  32.7 0.7 shard_map.96
  33.4 5.1 %collective-permute-start.1 = (f32[128,128]{1,0:T(8,128)S(1)}, f32[128,128]{1,0:T(8,128)S(1)}, u32[]{:S(2)}, u32[]{:S(2)}) collective-permute-start(f32[128,128]{1,0:T(8,128)S(1)} %get-tuple-element.42.refs_4_.refs_6_), channel_id=1, source_target_pairs={{0,1},{1,0},{2,3},{3,2},{4,5},{5,4},{6,7},{7,6},{8,9},{9,8},{10,11... | collective-permute-start | bytes 196616 | tf_op jit(solution)/shard_map/ppermute | solution.py:348
  38.6 0.9 %collective-permute-done.1.refs_5_.refs_7_ = f32[128,128]{1,0:T(8,128)S(1)} collective-permute-done((f32[128,128]{1,0:T(8,128)S(1)}, f32[128,128]{1,0:T(8,128)S(1)}, u32[]{:S(2)}, u32[]{:S(2)}) %collective-permute-start.1) | collective-permute-done | bytes 65568 | tf_op jit(solution)/shard_map/ppermute | solution.py:348
  39.5 1.0 %shard_map.97 = (bf16[128,3072]{1,0:T(8,128)(2,1)S(1)}, bf16[8,400,128]{2,1,0:T(8,128)(2,1)S(1)}) custom-call(f32[128,3072]{1,0:T(8,128)S(1)} %get-tuple-element.41.refs_0_.refs_4_, bf16[128,3072]{1,0:T(8,128)(2,1)S(1)} %copy-done.3, f32[24,128]{1,0:T(8,128)S(1)} %bitcast.9, bf16[128,3072]{1,0:T(8,128)(2,1)S(1)} %copy-done, ...), custom_call_target="tpu_custom_call" | custom-call | tf_op jit(solution)/shard_map/pallas_call | solution.py:23
  40.4 3.4 %shard_map.98 = (bf16[128,3072]{1,0:T(8,128)(2,1)S(1)}, f32[128,3072]{1,0:T(8,128)S(1)}, f32[128,3072]{1,0:T(8,128)S(1)}) custom-call(bf16[128,3072]{1,0:T(8,128)(2,1)S(1)} %copy-done, bf16[128,3072]{1,0:T(8,128)(2,1)S(1)} %copy-done.1, bf16[128,3072]{1,0:T(8,128)(2,1)S(1)} %get-tuple-element.58.refs_2_, bf16[128,3072]{1,0:T(8,128)(2,1)S(1)} %get-tuple-element.39.refs_3_), custom_call_target="tpu_custom_call" | custom-call | tf_op jit(solution)/shard_map/pallas_call | solution.py:100
  43.9 2.3 %shard_map.99 = (bf16[128,3072]{1,0:T(8,128)(2,1)}, bf16[128,3072]{1,0:T(8,128)(2,1)}) custom-call(bf16[128,3072]{1,0:T(8,128)(2,1)S(1)} %get-tuple-element.46.refs_0_, bf16[128,3072]{1,0:T(8,128)(2,1)S(1)} %copy-done.2, bf16[128,3072]{1,0:T(8,128)(2,1)S(1)} %get-tuple-element.58.refs_2_, bf16[3072,128]{1,0:T(8,128)(2,1)S(1)} %bitcast.5, ...), custom_call_target="tpu_custom_call" | custom-call | tf_op jit(solution)/shard_map/pallas_call | solution.py:100
  46.1 10.3 %all_to_all.22.got_ref.refs_0_ = bf16[8,400,128]{2,1,0:T(8,128)(2,1)S(1)} all-to-all(bf16[8,400,128]{2,1,0:T(8,128)(2,1)S(1)} %get-tuple-element.52), channel_id=1, replica_groups={{6,2,10,12,14,8,0,4},{22,18,26,28,30,24,16,20},{7,3,11,13,15,9,1,5},{23..., dimensions={0} | all-to-all | bytes 1638400 | tf_op jit(solution)/shard_map/all_to_all | solution.py:326
  56.4 0.1 shard_map.100
  56.5 3.7 %collective-permute-start.2 = (bf16[400,128]{1,0:T(8,128)(2,1)S(1)}, bf16[400,128]{1,0:T(8,128)(2,1)S(1)}, u32[]{:S(2)}, u32[]{:S(2)}) collective-permute-start(bf16[400,128]{1,0:T(8,128)(2,1)S(1)} %shard_map.100), channel_id=1, source_target_pairs={{0,16},{2,18},{4,20},{6,22},{8,24},{10,26},{12,28},{14,30},{16,0},... | collective-permute-start | bytes 307208 | tf_op jit(solution)/shard_map/ppermute | solution.py:334
  60.3 0.1 shard_map.102
  60.4 2.1 %collective-permute-done.2.refs_1_ = bf16[400,128]{1,0:T(8,128)(2,1)S(1)} collective-permute-done((bf16[400,128]{1,0:T(8,128)(2,1)S(1)}, bf16[400,128]{1,0:T(8,128)(2,1)S(1)}, u32[]{:S(2)}, u32[]{:S(2)}) %collective-permute-start.2) | collective-permute-done | bytes 102432 | tf_op jit(solution)/shard_map/ppermute | solution.py:334
  62.4 0.2 shard_map.103
  62.6 13.1 %all_to_all.23.refs_2_ = bf16[8,400,128]{2,1,0:T(8,128)(2,1)S(1)} all-to-all(bf16[8,400,128]{2,1,0:T(8,128)(2,1)S(1)} %shard_map.103), channel_id=1, replica_groups={{6,2,10,12,14,8,0,4},{22,18,26,28,30,24,16,20},{7,3,11,13,15,9,1,5},{23..., dimensions={0} | all-to-all | bytes 1638400 | tf_op jit(solution)/shard_map/all_to_all | solution.py:342
  75.7 2.2 %shard_map.104 = (bf16[128,3072]{1,0:T(8,128)(2,1)}, bf16[128,3072]{1,0:T(8,128)(2,1)}, f32[24,128]{1,0:T(8,128)}) custom-call(bf16[128,3072]{1,0:T(8,128)(2,1)S(1)} %copy-done.2, bf16[128,3072]{1,0:T(8,128)(2,1)S(1)} %copy-done.1, bf16[8,400,128]{2,1,0:T(8,128)(2,1)S(1)} %all_to_all.23.refs_2_, f32[128,3072]{1,0:T(8,128)S(1)} %get-tuple-element.56.refs_3_, ...), custom_call_target="tpu_custom_call" | custom-call | tf_op jit(solution)/shard_map/pallas_call | solution.py:100
  (9 shorter events, 0.0 us)
Async XLA Ops:
  2.4 16.8 %copy-start = (bf16[128,3072]{1,0:T(8,128)(2,1)S(1)}, bf16[128,3072]{1,0:T(8,128)(2,1)}, u32[]{:S(2)}) copy-start(bf16[128,3072]{1,0:T(8,128)(2,1)} %refs_0_.5) | copy-start | bytes 2359300
  2.4 16.7 %copy-start.1 = (bf16[128,3072]{1,0:T(8,128)(2,1)S(1)}, bf16[128,3072]{1,0:T(8,128)(2,1)}, u32[]{:S(2)}) copy-start(bf16[128,3072]{1,0:T(8,128)(2,1)} %refs_1_.15) | copy-start | bytes 2359300
  2.4 16.7 %copy-start.2 = (bf16[128,3072]{1,0:T(8,128)(2,1)S(1)}, bf16[128,3072]{1,0:T(8,128)(2,1)}, u32[]{:S(2)}) copy-start(bf16[128,3072]{1,0:T(8,128)(2,1)} %refs_0_.6) | copy-start | bytes 2359300
  16.8 5.5 %collective-permute-start = (bf16[384,128]{1,0:T(8,128)(2,1)S(1)}, bf16[384,128]{1,0:T(8,128)(2,1)S(1)}, u32[]{:S(2)}, u32[]{:S(2)}) collective-permute-start(bf16[384,128]{1,0:T(8,128)(2,1)S(1)} %shard_map.93), channel_id=1, source_target_pairs={{0,16},{2,18},{4,20},{6,22},{8,24},{10,26},{12,28},{14,30},{16,0},... | collective-permute-start | bytes 294920 | tf_op jit(solution)/shard_map/ppermute | solution.py:334
  20.1 12.6 %copy-start.3 = (bf16[128,3072]{1,0:T(8,128)(2,1)S(1)}, bf16[128,3072]{1,0:T(8,128)(2,1)}, u32[]{:S(2)}) copy-start(bf16[128,3072]{1,0:T(8,128)(2,1)} %refs_1_.10) | copy-start | bytes 2359300
  20.1 12.6 %copy-start.4 = (f32[3072]{0:T(1024)S(1)}, f32[3072]{0:T(1024)}, u32[]{:S(2)}) copy-start(f32[3072]{0:T(1024)} %param.8) | copy-start | bytes 36868
  33.4 6.0 %collective-permute-start.1 = (f32[128,128]{1,0:T(8,128)S(1)}, f32[128,128]{1,0:T(8,128)S(1)}, u32[]{:S(2)}, u32[]{:S(2)}) collective-permute-start(f32[128,128]{1,0:T(8,128)S(1)} %get-tuple-element.42.refs_4_.refs_6_), channel_id=1, source_target_pairs={{0,1},{1,0},{2,3},{3,2},{4,5},{5,4},{6,7},{7,6},{8,9},{9,8},{10,11... | collective-permute-start | bytes 196616 | tf_op jit(solution)/shard_map/ppermute | solution.py:348
  56.5 5.9 %collective-permute-start.2 = (bf16[400,128]{1,0:T(8,128)(2,1)S(1)}, bf16[400,128]{1,0:T(8,128)(2,1)S(1)}, u32[]{:S(2)}, u32[]{:S(2)}) collective-permute-start(bf16[400,128]{1,0:T(8,128)(2,1)S(1)} %shard_map.100), channel_id=1, source_target_pairs={{0,16},{2,18},{4,20},{6,22},{8,24},{10,26},{12,28},{14,30},{16,0},... | collective-permute-start | bytes 307208 | tf_op jit(solution)/shard_map/ppermute | solution.py:334
